TPU v7x, 512 devices: a whole 4x4x16 slice. The times are simulated.
512 devices in a mesh: seq: 64 (over z_lo, x, core), head: 8 (over z_hi, y).
Axes of the slice: x: 4, y: 4, z: 16 (z_hi: 2, z_lo: 8; z = z_hi * 8 + z_lo), core: 2. Of those that a mesh axis runs over, the one named last changes fastest.
Arguments:
- tokens: bfloat16 [8192, 3072], P('seq', 'head'), may hold values from -6 to 6
- qkv_weight: bfloat16 [3072, 6144], P('seq', 'head'), may hold values from -1 to 1
- qkv_bias: float32 [6144], P('head'), may hold values from -1.5 to 1.5
- q_gain: float32 [128], replicated, may hold values from 0.5 to 6.5
- k_gain: float32 [128], replicated, may hold values from 0.5 to 6.5
- cache_kv: bfloat16 [8192, 4096], P('seq', 'head'), may hold values from -127 to 127
- cache_scale: float32 [128, 16], P('seq', 'head'), may hold values from 0.008 to 0.03
- cache_code: int32 [128], P('seq'), may hold values from 0 to 1
- block_mask: int32 [128, 128], replicated, may hold values from 0 to 1, as said below
- out_weight: bfloat16 [2048, 3072], P('head', 'seq'), may hold values from -0.375 to 0.375
- out_bias: float32 [3072], P('head'), may hold values from -2.5 to 2.5
- out_gate: float32 [3072], P('head'), may hold values from -3 to 3
Outputs:
- attn_out: bfloat16 [8192, 3072], P('seq', 'head')
- block_mass: float32 [16, 128, 128], P('head', 'seq')
Inputs may be any that keep to these rules, and one draw needn't show every extreme that they name: Every block attends to itself: block_mask[b, b] = 1.
All inputs are finite; a program needn't handle non-finite values.
Results may differ from a plain program's by a relative error of at most 0.019.
The roundings to bfloat16 on the way count: a program that leaves them out, or rounds other values in their place, can miss the bound.
Values may be sent and summed in bfloat16 or wider, within the bound.
No kernel may reach another device: no remote copies, remote signals or barrier semaphores. Data moves between devices by JAX's collectives and lax.ppermute only.
A program may use at most 128 MiB of HBM per device.

v0:
```python
import math

import jax
import jax.numpy as jnp
from jax import lax
from jax.sharding import PartitionSpec as P

DH = 128
BLK = 64


def rms_scaled(vectors, gains):
    mean_square = jnp.mean(vectors * vectors, axis=-1, keepdims=True)
    return vectors * lax.rsqrt(mean_square + 1e-06) * gains


def per_device(
    tokens,
    qkv_weight,
    qkv_bias,
    q_gain,
    k_gain,
    cache_kv,
    cache_scale,
    cache_code,
    block_mask,
    out_weight,
    out_bias,
    out_gate,
):
    token_count = tokens.shape[0]
    local_heads = qkv_bias.shape[0] // (3 * DH)
    total_blocks = block_mask.shape[1]
    block_rows = token_count // BLK
    inv_root = 1.0 / math.sqrt(DH)
    seq_index = lax.axis_index("seq")
    own_mask = lax.dynamic_slice_in_dim(block_mask, seq_index * block_rows, block_rows, 0)
    full_tokens = lax.all_gather(tokens, "head", axis=1, tiled=True)
    projected = jnp.dot(
        full_tokens,
        lax.all_gather(qkv_weight, "seq", axis=0, tiled=True),
        preferred_element_type=jnp.float32,
    )
    projected = (projected + qkv_bias).reshape(token_count, local_heads, 3, DH)
    queries = rms_scaled(projected[:, :, 0], q_gain).astype(jnp.bfloat16)
    fresh_keys = rms_scaled(projected[:, :, 1], k_gain).astype(jnp.bfloat16)
    fresh_values = projected[:, :, 2].astype(jnp.bfloat16)
    cached = cache_kv.reshape(token_count, local_heads, 2, DH).astype(jnp.float32)
    factor = jnp.repeat(cache_scale, BLK, axis=0)[:, :, None]
    use_cache = (jnp.repeat(cache_code, BLK) == 1)[:, None, None]
    key_rows = jnp.where(use_cache, (cached[:, :, 0] * factor).astype(jnp.bfloat16), fresh_keys)
    value_rows = jnp.where(use_cache, (cached[:, :, 1] * factor).astype(jnp.bfloat16), fresh_values)
    packed = jnp.stack([key_rows, value_rows], axis=2).reshape(token_count, local_heads * 2 * DH)
    incoming = lax.all_gather(packed, "seq", axis=0, tiled=True)
    top_score = jnp.full((local_heads, token_count), -1e30, jnp.float32)
    query_count = queries.shape[0]
    piece_rows = incoming.shape[0]
    pairs = incoming.reshape(piece_rows, local_heads, 2, DH)
    scores = (
        jnp.einsum("qhd,khd->hqk", queries, pairs[:, :, 0], preferred_element_type=jnp.float32)
        * inv_root
    )
    allowed = (jnp.repeat(jnp.repeat(own_mask, BLK, axis=0), BLK, axis=1) == 1)[None]
    masked = jnp.where(allowed, scores, -1e30)
    new_top = jnp.maximum(top_score, jnp.max(masked, axis=2))
    exp_scores = jnp.where(allowed, jnp.exp(masked - new_top[:, :, None]), 0.0)
    totals = jnp.sum(exp_scores, axis=2)
    weighted = jnp.einsum(
        "hqk,khd->hqd",
        exp_scores.astype(jnp.bfloat16),
        pairs[:, :, 1],
        preferred_element_type=jnp.float32,
    )
    block_sums = exp_scores.reshape(local_heads, query_count, piece_rows // BLK, BLK).sum(axis=3)
    mass_rows = block_sums
    finished = (new_top, totals, weighted, mass_rows)
    top_score, totals, weighted, mass_rows = finished
    attended = (
        (weighted / totals[:, :, None])
        .transpose(1, 0, 2)
        .reshape(token_count, local_heads * DH)
        .astype(jnp.bfloat16)
    )
    block_mass = (
        (mass_rows / totals[:, :, None])
        .reshape(local_heads, token_count // BLK, BLK, total_blocks)
        .sum(axis=2)
    )
    partial_out = jnp.dot(
        attended,
        lax.all_gather(out_weight, "seq", axis=1, tiled=True),
        preferred_element_type=jnp.float32,
    )
    summed_out = lax.psum_scatter(
        partial_out.astype(jnp.bfloat16), "head", scatter_dimension=1, tiled=True
    ).astype(jnp.float32)
    attn_out = ((summed_out + out_bias) * out_gate).astype(jnp.bfloat16)
    return (attn_out, block_mass)


def solution(mesh):
    in_specs = (
        P("seq", "head"),
        P("seq", "head"),
        P("head"),
        P(),
        P(),
        P("seq", "head"),
        P("seq", "head"),
        P("seq"),
        P(),
        P("head", "seq"),
        P("head"),
        P("head"),
    )
    out_specs = (P("seq", "head"), P("head", "seq", None))
    return jax.shard_map(
        per_device, mesh=mesh, in_specs=in_specs, out_specs=out_specs, check_vma=False
    )
```

profile of v0, /device:TPU:6, one launch (start us, length us, event | category | flops | bytes accessed | tf_op | source)
XLA Modules:
  0.0 543.7 jit_solution(10314956427554896040)
XLA Ops:
  7.2 0.0 copy-start.3
  7.2 0.0 all-gather.4.cloned.1.call-start
  7.2 0.7 all-gather.4.cloned.1.call-update
  7.9 0.0 all-gather.6.cloned.1.call-start
  8.0 1.0 copy.47
  9.0 0.8 copy.48
  9.7 0.1 broadcast_in_dim.61
  9.8 0.1 mul.82
  9.9 0.7 broadcast_compare_fusion
  10.6 0.1 broadcast_in_dim.59
  10.6 0.1 eq.38
  10.7 79.6 %all_gather.12 = bf16[128,3072]{1,0:T(8,128)(2,1)S(1)} all-gather(bf16[128,384]{1,0:T(8,128)(2,1)} %param.12), channel_id=1, replica_groups=mesh['seq'=64,'head'=8] {'head'}, dimensions={1}, use_global_device_ids=true | all-gather | bytes 884736 | tf_op jit(solution)/shard_map/all_gather | solution.py:38
  90.3 48.0 %all-gather.4.cloned.1.call-done = bf16[3072,768]{1,0:T(8,128)(2,1)} async-done(((bf16[48,768]{1,0:T(8,128)(2,1)}), bf16[3072,768]{1,0:T(8,128)(2,1)}) %all-gather.4.cloned.1.call-update) | async-done | bytes 4718608 | tf_op jit(solution)/shard_map/all_gather | solution.py:41
  138.3 3.1 convolution_add_fusion
  141.4 0.2 copy.46
  141.6 0.7 fusion.14
  142.4 0.7 pad_maximum_fusion
  143.1 0.0 all-gather.6.cloned.1.call-update
  143.1 0.0 all-gather.8.cloned.1.call-start
  143.1 0.7 all-gather.8.cloned.1.call-update
  143.8 0.0 reduce-scatter.4.cloned.1.call-start
  143.9 0.7 dynamic-slice_compare_fusion
  144.6 0.1 copy.44
  144.7 0.3 broadcast_in_dim.57
  145.0 2.3 copy.45
  147.3 151.4 %all-gather.6.cloned.1.call-done = bf16[8192,512]{0,1:T(8,128)(2,1)} async-done(((bf16[128,512]{0,1:T(8,128)(2,1)}), bf16[8192,512]{0,1:T(8,128)(2,1)}) %all-gather.6.cloned.1.call-update) | async-done | bytes 8388624 | tf_op jit(solution)/shard_map/all_gather | solution.py:54
  298.8 0.0 copy-done.3
  298.8 4.3 fusion.19
  303.1 2.7 fusion.18
  305.8 0.0 copy-start
  305.8 3.2 copy-done
  309.0 3.6 fusion.9
  312.6 104.7 %all-gather.8.cloned.1.call-done = bf16[256,3072]{0,1:T(8,128)(2,1)} async-done(((bf16[256,48]{0,1:T(8,128)(2,1)}), bf16[256,3072]{0,1:T(8,128)(2,1)}) %all-gather.8.cloned.1.call-update) | async-done | bytes 1572880 | tf_op jit(solution)/shard_map/all_gather | solution.py:91
  417.4 2.1 convolution_convert_fusion
  419.4 1.2 copy.55
  420.6 0.0 reduce-scatter.4.cloned.1.call-update
  420.6 8.9 %copy.52 = f32[2,128,8192]{1,2,0:T(8,128)} copy(f32[2,128,8192]{2,1,0:T(8,128)} %copy-done) | data formatting | bytes 16777216 | tf_op jit(solution)/shard_map/jit(_where)/select_n | solution.py:66
  429.5 0.0 copy-start.1
  429.5 0.0 copy-start.2
  429.5 0.1 div.33
  429.6 4.7 bitcast_reduce_fusion
  434.3 0.1 copy.53
  434.4 0.7 divide_reduce_fusion
  435.1 100.3 %reduce-scatter.4.cloned.1.call-done = bf16[384,128]{1,0:T(8,128)(2,1)} async-done(((bf16[3072,128]{1,0:T(8,128)(2,1)}), bf16[384,128]{1,0:T(8,128)(2,1)}) %reduce-scatter.4.cloned.1.call-update) | async-done | bytes 98320
  535.5 1.0 copy.56
  536.5 0.0 copy-done.1
  536.5 0.0 copy-done.2
  536.5 0.7 multiply_convert_fusion
  (6 shorter events, 0.1 us)
Async XLA Ops:
  7.2 291.6 %copy-start.3 = (f32[128]{0:T(128)S(1)}, f32[128]{0:T(128)}, u32[]{:S(2)}) copy-start(f32[128]{0:T(128)} %param.15) | copy-start | bytes 1540
  7.2 131.1 %all-gather.4.cloned.1.call-start = ((), (), s32[]{:S(2)}) async-start(), calls=%async_computation.1 | async-start | bytes 4792320 | tf_op jit(solution)/shard_map/all_gather | solution.py:41
  7.9 290.9 %all-gather.6.cloned.1.call-start = ((), (), s32[]{:S(2)}) async-start(), calls=%async_computation.2 | async-start | bytes 8519680 | tf_op jit(solution)/shard_map/all_gather | solution.py:54
  143.1 274.3 %all-gather.8.cloned.1.call-start = ((), (), s32[]{:S(2)}) async-start(), calls=%async_computation.3 | async-start | bytes 1597440 | tf_op jit(solution)/shard_map/all_gather | solution.py:91
  143.8 391.7 %reduce-scatter.4.cloned.1.call-start = ((), (), s32[]{:S(2)}) async-start(), calls=%async_computation.4 | async-start | bytes 884736
  305.8 3.2 copy-start
  429.5 107.0 %copy-start.1 = (f32[384]{0:T(512)S(1)}, f32[384]{0:T(512)}, u32[]{:S(2)}) copy-start(f32[384]{0:T(512)} %param.23) | copy-start | bytes 4612
  429.5 107.0 %copy-start.2 = (f32[384]{0:T(512)S(1)}, f32[384]{0:T(512)}, u32[]{:S(2)}) copy-start(f32[384]{0:T(512)} %param.22) | copy-start | bytes 4612
Sparse Core Ops, SparseCore 0:
  10.2 128.0 all-gather.3
  143.2 155.5 all-gather.5
  300.9 116.4 all-gather.7
  421.7 113.7 reduce-scatter.3
where the time goes:
time: 544 us
  waiting for transfers between devices  406 us (75%)
  blocking collectives  79.6 us (15%)
  local copies, waits for them, and re-layouts  19.4 us (4%)
  between operations  13.9 us (3%)
  matrix products  13.1 us (2%)
  other arithmetic  11.6 us (2%)
    all_gather x1, waiting for transfers between devices, per_device(): incoming = lax.all_gather(packed, 'seq', axis=0, tiled=True)  151 us
    all_gather x1, waiting for transfers between devices, per_device(): lax.all_gather(out_weight, 'seq', axis=1, tiled=True)  105 us
    unnamed x5, waiting for transfers between devices  102 us
    all_gather x1, blocking collectives, per_device(): full_tokens = lax.all_gather(tokens, 'head', axis=1, tiled=True)  79.6 us
    all_gather x1, waiting for transfers between devices, per_device(): lax.all_gather(qkv_weight, 'seq', axis=0, tiled=True)  48 us
  transfers between devices with their start and end apart: 4, of which 4 were waited for; matrix products, arithmetic and copies ran while one was open for 6% of the time, Pallas kernels for 0%

commit v1 on v0

v1 whole, which is shorter than its diff:
```python
import functools
import math

import jax
import jax.numpy as jnp
from jax import lax
from jax.experimental import pallas as pl
from jax.experimental.pallas import tpu as pltpu
from jax.sharding import Mesh, PartitionSpec as P

BF = jnp.bfloat16
F32 = jnp.float32
DH = 128
FRESH = 1e30
FLOOR = -1e29
SHUT = -1e30
LOG2E = 1.4426950408889634

VM = pl.BlockSpec(memory_space=pltpu.VMEM)
SM = pl.BlockSpec(memory_space=pltpu.SMEM)


def call(kernel, outs, n_in, n_smem, scratch=(), flops=0, name=None):
    multiple = isinstance(outs, (list, tuple))
    return pl.pallas_call(
        kernel,
        out_shape=outs,
        in_specs=[SM] * n_smem + [VM] * (n_in - n_smem),
        out_specs=[VM] * len(outs) if multiple else VM,
        scratch_shapes=list(scratch),
        compiler_params=pltpu.CompilerParams(vmem_limit_bytes=48 * 1024 * 1024),
        name=name,
    )


def nt(a, b, precision=None):
    return lax.dot_general(
        a, b, (((1,), (1,)), ((), ())), preferred_element_type=F32, precision=precision
    )


def tn(a, b):
    return lax.dot_general(a, b, (((0,), (0,)), ((), ())), preferred_element_type=F32)


def prep_kernel(pos, scale, code, w_ref, cache_ref, tok_ref, ot_ref, keep_ref, send_ref, first_ref):
    zh = pos[0]
    for t in range(3):
        a = w_ref[:, t * 128 : (t + 1) * 128]
        b = w_ref[:, 384 + t * 128 : 384 + (t + 1) * 128]
        keep_ref[t * 48 : (t + 1) * 48, :] = jnp.where(zh == 0, a, b)
        send_ref[t * 48 : (t + 1) * 48, :] = jnp.where(zh == 0, b, a)
    for part in range(2):
        for blk in range(2):
            rows = slice(blk * 64, blk * 64 + 64)
            at = slice(144 + part * 128 + blk * 64, 144 + part * 128 + blk * 64 + 64)
            both = []
            for j in range(2):
                raw = cache_ref[rows, j * 256 + part * 128 : j * 256 + part * 128 + 128]
                row = (raw.astype(F32) * scale[blk, j]).astype(BF)
                both.append(jnp.where(code[blk] == 1, row, jnp.full_like(row, FRESH)))
            keep_ref[at, :] = jnp.where(zh == 0, both[0], both[1])
            send_ref[at, :] = jnp.where(zh == 0, both[1], both[0])
    for f in range(3):
        first_ref[f * 128 : (f + 1) * 128, :] = tok_ref[:, f * 128 : (f + 1) * 128]
    for j in range(2):
        first_ref[384 + j * 48 : 384 + (j + 1) * 48, :] = ot_ref[:, j * 128 : (j + 1) * 128]


def project_kernel(
    pos, x0, x1, x2, x3, wown, woth, bias, qg, kg, keep, recv, q_ref, kv_ref
):
    zh, c, y = pos[0], pos[1], pos[2]
    total = jnp.zeros((256, 384), F32)
    for k, xr in enumerate((x0, x1, x2, x3)):
        yy = lax.rem(y + (4 - k), 4)
        for w in range(2):
            slot = jnp.where(zh == 0, w, 1 - w)
            rows = []
            for z in range(2):
                rows.append(jnp.concatenate([xr[w * 2 + z, f * 128 : (f + 1) * 128, :] for f in range(3)], axis=1))
            x = jnp.concatenate(rows, axis=0)
            pieces = []
            for xx in range(4):
                own = jnp.concatenate([wown[xx, yy, slot, t * 48 : (t + 1) * 48, :] for t in range(3)], axis=1)
                oth = jnp.concatenate([woth[xx, yy, slot, t * 48 : (t + 1) * 48, :] for t in range(3)], axis=1)
                pieces.append(jnp.where(c == 0, own, oth))
                pieces.append(jnp.where(c == 0, oth, own))
            total = total + jnp.dot(x, jnp.concatenate(pieces, axis=0), preferred_element_type=F32)
    total = total + jnp.where(zh == 0, bias[:, :384], bias[:, 384:])

    def scaled(v, gain):
        ms = jnp.mean(v * v, axis=-1, keepdims=True)
        return (v * lax.rsqrt(ms + 1e-06) * gain).astype(BF)

    q_ref[...] = scaled(total[:, :128], qg[...])
    fresh = (scaled(total[:, 128:256], kg[...]), total[:, 256:].astype(BF))
    for part in range(2):
        at = slice(144 + part * 128, 144 + part * 128 + 128)
        a, b = keep[at, :], recv[at, :]
        for z in range(2):
            cached = jnp.where(zh == z, a, b)
            new = fresh[part][z * 128 : (z + 1) * 128]
            kv_ref[part * 256 + z * 128 : part * 256 + (z + 1) * 128, :] = jnp.where(
                cached.astype(F32) < 1e29, cached, new
            )


def attend_kernel(q_ref, kv0, kv1, mask_ref, out_ref, s_ref):
    unit = LOG2E / math.sqrt(DH)
    q = jnp.concatenate([q_ref[i] for i in range(4)], axis=0)
    top = jnp.full((1, 1024), FLOOR, F32)
    for ch in range(8):
        kv = (kv0, kv1)[ch // 4]
        s = nt(kv[ch % 4, :256, :], q) * unit
        for b in range(4):
            row = ch * 4 + b
            open_ = mask_ref[row : row + 1, :] > 0
            sb = jnp.where(open_, s[b * 64 : (b + 1) * 64], SHUT)
            s_ref[ch * 256 + b * 64 : ch * 256 + (b + 1) * 64, :] = sb
            top = jnp.maximum(top, jnp.max(sb, axis=0, keepdims=True))
    total = jnp.zeros((1, 1024), F32)
    out = jnp.zeros((128, 1024), F32)
    mass = []
    for ch in range(8):
        kv = (kv0, kv1)[ch // 4]
        p = jnp.exp2(s_ref[ch * 256 : (ch + 1) * 256, :] - top)
        for b in range(4):
            row = jnp.sum(p[b * 64 : (b + 1) * 64], axis=0, keepdims=True)
            mass.append(row)
            total = total + row
        out = out + tn(kv[ch % 4, 256:, :], p.astype(BF))
    for i in range(4):
        cols = slice(i * 256, (i + 1) * 256)
        out_ref[i, :128, :] = out[:, cols]
        for r in range(32):
            out_ref[i, 128 + r : 129 + r, :] = mass[r][:, cols]
        out_ref[i, 160:161, :] = top[:, cols]
        out_ref[i, 161:162, :] = total[:, cols]
        out_ref[i, 162:168, :] = jnp.zeros((6, 256), F32)


def merge_kernel(pos, parts, out_ref):
    c = pos[1]
    hi = lax.Precision.HIGHEST
    tops = [parts[i, 160:161, :] for i in range(4)]
    top = jnp.maximum(jnp.maximum(tops[0], tops[1]), jnp.maximum(tops[2], tops[3]))
    factors = [jnp.exp2(t - top) for t in tops]
    total = sum(f * parts[i, 161:162, :] for i, f in enumerate(factors))
    shares = [f / total for f in factors]
    out = sum(s * parts[i, :128, :] for i, s in enumerate(shares))
    att = out.T.astype(BF)
    mass = jnp.concatenate([s * parts[i, 128:160, :] for i, s in enumerate(shares)], axis=0)
    i = lax.broadcasted_iota(jnp.int32, (128, 128), 0)
    b = lax.broadcasted_iota(jnp.int32, (128, 128), 1)
    cc = jnp.bitwise_xor((i >> 4) & 1, c)
    place = ((i >> 1) & 1) * 64 + ((i >> 2) & 3) * 16 + (i >> 5) * 4 + cc * 2 + (i & 1)
    order = (place == b).astype(F32)
    r = lax.broadcasted_iota(jnp.int32, (16, 256), 0)
    t = lax.broadcasted_iota(jnp.int32, (16, 256), 1)
    row = lax.broadcasted_iota(jnp.int32, (16, 128), 0)
    for z in range(2):
        pick = ((r < 6) & ((t >> 6) == z * 2 + (r & 1))).astype(F32)
        m = jnp.dot(nt(pick, mass, hi), order, preferred_element_type=F32, precision=hi)
        a = m.astype(BF).astype(F32)
        d = (m - a).astype(BF).astype(F32)
        e = m - a - d
        packed = jnp.where(row < 2, a, jnp.where(row < 4, d, jnp.where(row < 6, e, 0.0))).astype(BF)
        for w in range(2):
            out_ref[w * 2 + z, :128, :] = att[z * 128 : (z + 1) * 128]
            out_ref[w * 2 + z, 128:144, :] = packed


def finish_kernel(pos, att, got, oown, ooth, bias, gate, out_ref, mass_ref):
    c, w = pos[1], pos[3]
    cols, weights = [], []
    for y in range(4):
        for ww in range(2):
            for j in range(2):
                cols.append(att[y, ww * 2 + j])
    a = jnp.concatenate(cols, axis=1)
    for x in range(4):
        own = jnp.concatenate(
            [oown[x, y, ww, j * 48 : (j + 1) * 48, :] for y in range(4) for ww in range(2) for j in range(2)], axis=1
        )
        oth = jnp.concatenate(
            [ooth[x, y, ww, j * 48 : (j + 1) * 48, :] for y in range(4) for ww in range(2) for j in range(2)], axis=1
        )
        weights.append(jnp.where(c == 0, own, oth))
        weights.append(jnp.where(c == 0, oth, own))
    total = nt(a, jnp.concatenate(weights, axis=0))
    out_ref[...] = ((total + bias[...]) * gate[...]).astype(BF)
    for j in range(2):
        r = got[w * 2 + j, 128:144, :].astype(F32)
        mass_ref[j] = r[0:2] + r[2:4] + r[4:6]


def swap(v, axis):
    return lax.ppermute(v, axis, [(0, 1), (1, 0)])


def turn(v, axis, k):
    return lax.ppermute(v, axis, [(i, (i + k) % 4) for i in range(4)])


def per_device(
    tokens, qkv_weight, qkv_bias, q_gain, k_gain, cache_kv, cache_scale, cache_code, block_mask, out_weight,
    out_bias, out_gate,
):
    zh, zl, x, c, w, y = (lax.axis_index(n) for n in ("zh", "zl", "x", "c", "w", "y"))
    pos = jnp.stack([zh, c, y, w]).astype(jnp.int32)
    sd = jax.ShapeDtypeStruct

    keep, send, first = call(
        prep_kernel, [sd((400, 128), BF), sd((400, 128), BF), sd((480, 128), BF)], 7, 3, name="prep"
    )(pos, cache_scale, cache_code, qkv_weight, cache_kv, tokens, out_weight.T)

    recv = swap(send, "zh")
    spread = lax.all_gather(first, ("w", "zh"), axis=0, tiled=False)
    toks = spread[:, :384]
    outs = lax.dynamic_index_in_dim(spread[:, 384:].reshape(2, 2, 96, 128), w, 1, keepdims=False)
    second = jnp.concatenate([keep[:144], recv[:144], outs.reshape(192, 128)], axis=0)
    along = lax.all_gather(second, "zl", axis=0, tiled=False)
    x1, x2, x3 = (turn(toks, "y", k) for k in (1, 2, 3))
    wts = along[:, :288].reshape(4, 2, 144, 128)
    wa = lax.all_gather(wts[:2], "x", axis=0, tiled=False)
    wb = lax.all_gather(wts[2:], "x", axis=0, tiled=False)
    wown = jnp.concatenate([wa, wb], axis=1)
    woth = swap(wown, "c")
    ow = lax.all_to_all(along[:, 288:], "y", 0, 0, tiled=True)

    q, kv = call(
        project_kernel, [sd((256, 128), BF), sd((512, 128), BF)], 12, 1, name="project"
    )(pos, toks, x1, x2, x3, wown, woth, qkv_bias[None], q_gain[None], k_gain[None], keep, recv)

    kv0 = lax.all_gather(kv, "zl", axis=0, tiled=False)
    kv1 = swap(kv0, "c")
    qs = lax.all_to_all(jnp.broadcast_to(q[None], (4, 256, 128)), "x", 0, 0, tiled=True)

    bm = block_mask.reshape(2, 4, 4, 2, 2, 2, 4, 4, 2, 2)
    zero = jnp.zeros((), jnp.int32)
    bm = lax.dynamic_slice(
        bm, (zero, zl, zero, c, zero, zero, zero, x, zero, zero), (2, 1, 4, 1, 2, 2, 4, 1, 2, 2)
    ).reshape(2, 4, 2, 2, 4, 2, 2)
    bm = jnp.where(c == 0, bm, bm[:, :, :, :, :, ::-1])
    bm = bm.transpose(5, 4, 3, 6, 1, 0, 2).reshape(32, 16)
    mask = jnp.repeat(bm.astype(F32), 64, axis=1)

    parts = call(
        attend_kernel, sd((4, 168, 256), F32), 4, 0, [pltpu.VMEM((2048, 1024), F32)], name="attend"
    )(qs, kv0, kv1, mask)
    parts = lax.all_to_all(parts, "x", 0, 0, tiled=True)
    done = call(merge_kernel, sd((4, 144, 128), BF), 2, 1, name="merge")(pos, parts)
    got = lax.all_to_all(done, ("w", "zh"), 0, 0, tiled=True)
    att = lax.all_gather(got[:, :128], "y", axis=0, tiled=False)

    oown = lax.all_gather(ow.reshape(4, 2, 96, 128), "x", axis=0, tiled=False)
    ooth = swap(oown, "c")
    return call(
        finish_kernel, [sd((128, 384), BF), sd((2, 2, 128), F32)], 7, 1, name="finish"
    )(pos, att, got, oown, ooth, out_bias[None], out_gate[None])


def solution(mesh):
    split = Mesh(mesh.devices.reshape(2, 4, 4, 2, 2, 4), ("zh", "zl", "x", "c", "w", "y"))
    seq, head = ("zh", "zl", "x", "c"), ("w", "y")
    in_specs = (
        P(seq, head), P(seq, head), P(head), P(), P(), P(seq, head), P(seq, head), P(seq), P(), P(head, seq),
        P(head), P(head),
    )
    out_specs = (P(seq, head), P(head, seq, None))
    return jax.shard_map(per_device, mesh=split, in_specs=in_specs, out_specs=out_specs, check_vma=False)
```

time: 544 us -> 234 us (0.43)
  waiting for transfers between devices: 406 us -> 28.3 us
  blocking collectives: 79.6 us -> 127 us
  starting transfers between devices: 0.16 us -> 47.1 us
  matrix products: 13.1 us -> 0 us
  between operations: 13.9 us -> 0.89 us
  other arithmetic: 11.6 us -> 0.1 us
  Pallas kernels: 0 us -> 11.2 us
    all_gather x3 -> x0, waiting for transfers between devices: 304 us -> none  [the longest x1 151 us: per_device(): incoming = lax.all_gather(packed, 'seq', axis=0, tiled=True)]
    unnamed x5 -> x0, waiting for transfers between devices: 102 us -> none
    all_gather x1 -> x7, blocking collectives: 79.6 us -> 127 us  [the longest x1 37.3 us: per_device(): spread = lax.all_gather(first, ('w', 'zh'), axis=0, tiled=False)]
    ppermute x0 -> x7, starting transfers between devices: none -> 26.4 us  [the longest x4 14.8 us: swap(): return lax.ppermute(v, axis, [(0, 1), (1, 0)])]
    all_to_all x0 -> x4, starting transfers between devices: none -> 20.7 us  [the longest x1 7.02 us: per_device(): got = lax.all_to_all(done, ('w', 'zh'), 0, 0, tiled=True)]
    all_to_all x0 -> x4, waiting for transfers between devices: none -> 14.3 us  [the longest x1 13.8 us: per_device(): got = lax.all_to_all(done, ('w', 'zh'), 0, 0, tiled=True)]
    ppermute x0 -> x7, waiting for transfers between devices: none -> 14.1 us  [the longest x3 14.1 us: turn(): return lax.ppermute(v, axis, [(i, (i + k) % 4) for i in range(4)])]
    dot_general x4 -> x0, matrix products: 13.1 us -> none  [the longest x1 4.28 us: per_device(): jnp.einsum('qhd,khd->hqk', queries, pairs[:, :, 0], preferred_element_typ...]
  transfers between devices with their start and end apart: 4 -> 11, of which waited for: 4 -> 5; matrix products, arithmetic and copies ran while one was open for 6% -> 5% of each run, Pallas kernels for 0% -> 3%
where the time goes in v1:
time: 234 us; the launch traced here: 231 us
  blocking collectives  127 us (54%)
  starting transfers between devices  47.1 us (20%)
  waiting for transfers between devices  28.3 us (12%)
  local copies, waits for them, and re-layouts  16.5 us (7%)
  Pallas kernels  11.2 us (5%)
    all_gather x1, blocking collectives, per_device(): spread = lax.all_gather(first, ('w', 'zh'), axis=0, tiled=False)  37.3 us
    all_gather x1, blocking collectives, per_device(): oown = lax.all_gather(ow.reshape(4, 2, 96, 128), 'x', axis=0, tiled=False)  18.1 us
    all_gather x1, blocking collectives, per_device(): kv0 = lax.all_gather(kv, 'zl', axis=0, tiled=False)  16 us
    all_gather x1, blocking collectives, per_device(): along = lax.all_gather(second, 'zl', axis=0, tiled=False)  14.9 us
    ppermute x4, starting transfers between devices, swap(): return lax.ppermute(v, axis, [(0, 1), (1, 0)])  14.8 us
    ppermute x3, waiting for transfers between devices, turn(): return lax.ppermute(v, axis, [(i, (i + k) % 4) for i in range(4)])  14.1 us
    all_to_all x1, waiting for transfers between devices, per_device(): got = lax.all_to_all(done, ('w', 'zh'), 0, 0, tiled=True)  13.8 us
    all_gather x1, blocking collectives, per_device(): att = lax.all_gather(got[:, :128], 'y', axis=0, tiled=False)  13.8 us
  transfers between devices with their start and end apart: 11, of which 5 were waited for; matrix products, arithmetic and copies ran while one was open for 5% of the time, Pallas kernels for 3%

profile of v1, /device:TPU:6, one launch (start us, length us, event | category | flops | bytes accessed | tf_op | source)
XLA Modules:
  0.0 230.9 jit_solution(9569058151030390313)
XLA Ops:
  0.6 0.1 pad_add_fusion.pos
  0.7 0.0 copy-start
  0.7 0.9 copy-done
  1.6 0.0 copy-start.1
  1.6 0.9 copy-done.1
  2.5 0.0 copy-start.2
  2.5 0.9 copy-done.2
  3.4 0.7 copy-done.3
  4.1 0.7 copy-done.4
  4.8 0.7 copy-done.5
  5.5 0.6 prep.1
  6.1 9.1 %collective-permute-start.3 = (bf16[400,128]{1,0:T(8,128)(2,1)S(1)}, bf16[400,128]{1,0:T(8,128)(2,1)S(1)}, u32[]{:S(2)}, u32[]{:S(2)}) collective-permute-start(bf16[400,128]{1,0:T(8,128)(2,1)S(1)} %get-tuple-element.9), channel_id=1, source_target_pairs={{0,256},{256,0},{1,257},{257,1},{2,258},{258,2},{3,259},{259,3},{4... | collective-permute-start | bytes 307208 | tf_op jit(solution)/shard_map/ppermute | solution.py:199
  15.2 37.3 %all-gather = bf16[1920,128]{1,0:T(8,128)(2,1)S(1)} all-gather(bf16[480,128]{1,0:T(8,128)(2,1)S(1)} %get-tuple-element.7), channel_id=2, replica_groups=mesh['zh'=2,'zl'=4,'x'=4,'c'=2,'w'=2,'y'=4] {'w','zh'}, dimensions={0}, use_global_device_ids=true | all-gather | bytes 614400 | tf_op jit(solution)/shard_map/all_gather | solution.py:219
  52.6 0.0 collective-permute-done.3.recv
  52.6 14.9 %all-gather.1 = bf16[1920,128]{1,0:T(8,128)(2,1)S(1)} all-gather(bf16[480,128]{1,0:T(8,128)(2,1)S(1)} %pad_maximum_fusion), channel_id=3, replica_groups=mesh['zh'=2,'zl'=4,'x'=4,'c'=2,'w'=2,'y'=4] {'zl'}, dimensions={0}, use_global_device_ids=true | all-gather | bytes 614400 | tf_op jit(solution)/shard_map/all_gather | solution.py:223
  67.5 13.5 %all_gather.44 = bf16[4,2,2,144,128]{4,3,2,1,0:T(8,128)(2,1)S(1)} all-gather(bf16[1,2,2,144,128]{4,3,2,1,0:T(8,128)(2,1)S(1)} %bitcast.31), channel_id=1, replica_groups=mesh['zh'=2,'zl'=4,'x'=4,'c'=2,'w'=2,'y'=4] {'x'}, dimensions={0}, use_global_device_ids=true | all-gather | bytes 737280 | tf_op jit(solution)/shard_map/all_gather | solution.py:226
  81.1 0.0 copy-start.9
  81.1 0.0 copy-start.6
  81.2 0.0 copy-start.7
  81.2 13.0 %all_gather.46 = bf16[4,2,2,144,128]{4,3,2,1,0:T(8,128)(2,1)S(1)} all-gather(bf16[1,2,2,144,128]{4,3,2,1,0:T(8,128)(2,1)S(1)} %bitcast.30), channel_id=1, replica_groups=mesh['zh'=2,'zl'=4,'x'=4,'c'=2,'w'=2,'y'=4] {'x'}, dimensions={0}, use_global_device_ids=true | all-gather | bytes 737280 | tf_op jit(solution)/shard_map/all_gather | solution.py:227
  94.2 0.1 constant_dynamic-update-slice_fusion.wown
  94.3 1.9 collective-permute-start.4
  96.3 3.5 %collective-permute-start = (bf16[4,384,128]{2,1,0:T(8,128)(2,1)S(1)}, bf16[4,384,128]{2,1,0:T(8,128)(2,1)S(1)}, u32[]{:S(2)}, u32[]{:S(2)}) collective-permute-start(bf16[4,384,128]{2,1,0:T(8,128)(2,1)S(1)} %slice.37.x0), channel_id=1, source_target_pairs={{0,1},{1,2},{2,3},{3,0},{4,5},{5,6},{6,7},{7,4},{8,9},{9,10},{10,1... | collective-permute-start | bytes 1179656 | tf_op jit(solution)/shard_map/ppermute | solution.py:203
  99.8 4.8 %collective-permute-start.1 = (bf16[4,384,128]{2,1,0:T(8,128)(2,1)S(1)}, bf16[4,384,128]{2,1,0:T(8,128)(2,1)S(1)}, u32[]{:S(2)}, u32[]{:S(2)}) collective-permute-start(bf16[4,384,128]{2,1,0:T(8,128)(2,1)S(1)} %slice.37.x0), channel_id=1, source_target_pairs={{0,2},{1,3},{2,0},{3,1},{4,6},{5,7},{6,4},{7,5},{8,10},{9,11},{10,... | collective-permute-start | bytes 1179656 | tf_op jit(solution)/shard_map/ppermute | solution.py:203
  104.6 3.3 %collective-permute-start.2 = (bf16[4,384,128]{2,1,0:T(8,128)(2,1)S(1)}, bf16[4,384,128]{2,1,0:T(8,128)(2,1)S(1)}, u32[]{:S(2)}, u32[]{:S(2)}) collective-permute-start(bf16[4,384,128]{2,1,0:T(8,128)(2,1)S(1)} %slice.37.x0), channel_id=1, source_target_pairs={{0,3},{1,0},{2,1},{3,2},{4,7},{5,4},{6,5},{7,6},{8,11},{9,8},{10,9... | collective-permute-start | bytes 1179656 | tf_op jit(solution)/shard_map/ppermute | solution.py:203
  107.8 0.0 copy-done.9
  107.9 3.1 %collective-permute-done.x1 = bf16[4,384,128]{2,1,0:T(8,128)(2,1)S(1)} collective-permute-done((bf16[4,384,128]{2,1,0:T(8,128)(2,1)S(1)}, bf16[4,384,128]{2,1,0:T(8,128)(2,1)S(1)}, u32[]{:S(2)}, u32[]{:S(2)}) %collective-permute-start) | collective-permute-done | bytes 393248 | tf_op jit(solution)/shard_map/ppermute | solution.py:203
  111.0 9.6 %collective-permute-done.1.x2 = bf16[4,384,128]{2,1,0:T(8,128)(2,1)S(1)} collective-permute-done((bf16[4,384,128]{2,1,0:T(8,128)(2,1)S(1)}, bf16[4,384,128]{2,1,0:T(8,128)(2,1)S(1)}, u32[]{:S(2)}, u32[]{:S(2)}) %collective-permute-start.1) | collective-permute-done | bytes 393248 | tf_op jit(solution)/shard_map/ppermute | solution.py:203
  120.5 1.4 collective-permute-done.2.x3
  121.9 0.0 collective-permute-done.4.woth
  121.9 0.0 copy-done.6
  121.9 0.0 copy-done.7
  121.9 1.8 project.1
  123.7 0.0 copy-start.8
  123.7 16.0 %all-gather.2 = bf16[2048,128]{1,0:T(8,128)(2,1)S(1)} all-gather(bf16[512,128]{1,0:T(8,128)(2,1)S(1)} %get-tuple-element.11), channel_id=4, replica_groups=mesh['zh'=2,'zl'=4,'x'=4,'c'=2,'w'=2,'y'=4] {'zl'}, dimensions={0}, use_global_device_ids=true | all-gather | bytes 655360 | tf_op jit(solution)/shard_map/all_gather | solution.py:236
  139.8 1.9 collective-permute-start.5
  141.7 0.7 broadcast_in_dim.27
  142.4 4.5 %all-to-all-start = ((bf16[4,256,128]{2,1,0:T(8,128)(2,1)}), bf16[4,256,128]{2,1,0:T(8,128)(2,1)S(1)}, u32[]{:S(2)}, u32[]{:S(2)}) async-start(bf16[4,256,128]{2,1,0:T(8,128)(2,1)} %broadcast_in_dim.27), calls=%async_computation | async-start | bytes 524288 | tf_op jit(solution)/shard_map/all_to_all | solution.py:238
  146.9 0.0 copy-done.8
  146.9 7.7 %reshape.30 = s32[2,4,4,2,2,2,4,4,2,2]{9,8,7,6,5,4,3,2,1,0:T(2,128)} reshape(s32[128,128]{1,0:T(8,128)S(1)} %copy-done.8) | data formatting | bytes 131072 | tf_op jit(solution)/shard_map/reshape | solution.py:240
  154.7 0.9 constant_dynamic-slice_fusion
  155.6 0.5 copy.17
  156.1 0.7 slice.43
  156.8 0.0 all-to-all-done.q_ref
  156.8 4.4 %all-to-all-start.3 = ((bf16[4,192,128]{2,1,0:T(8,128)(2,1)}), bf16[4,192,128]{2,1,0:T(8,128)(2,1)S(1)}, u32[]{:S(2)}, u32[]{:S(2)}) async-start(bf16[4,192,128]{2,1,0:T(8,128)(2,1)} %slice.43), calls=%async_computation.3 | async-start | bytes 393216 | tf_op jit(solution)/shard_map/all_to_all | solution.py:230
  161.2 0.6 copy.20
  161.7 0.2 reshape.37
  161.9 0.1 broadcast_in_dim.28
  162.0 0.1 reshape.32.mask_ref
  162.2 0.0 collective-permute-done.5.kv1
  162.2 4.8 %attend.1 = f32[4,168,256]{2,1,0:T(8,128)} custom-call(bf16[4,256,128]{2,1,0:T(8,128)(2,1)S(1)} %all-to-all-done.q_ref, bf16[4,512,128]{2,1,0:T(8,128)(2,1)S(1)} %bitcast.20, bf16[4,512,128]{2,1,0:T(8,128)(2,1)S(1)} %collective-permute-done.5.kv1, f32[32,1024]{1,0:T(8,128)S(1)} %reshape.32.mask_ref), custom_call_target="tpu_custom_call" | custom-call | tf_op jit(solution)/shard_map/attend/pallas_call | solution.py:249
  167.0 0.4 all-to-all-done.3
  167.5 4.8 %all-to-all-start.1 = ((f32[4,168,256]{2,1,0:T(8,128)}), f32[4,168,256]{2,1,0:T(8,128)S(1)}, u32[]{:S(2)}, u32[]{:S(2)}) async-start(f32[4,168,256]{2,1,0:T(8,128)} %attend.1), calls=%async_computation.1 | async-start | bytes 1376256 | tf_op jit(solution)/shard_map/all_to_all | solution.py:252
  172.3 18.1 %all_gather.51.oown = bf16[4,4,2,96,128]{4,3,2,1,0:T(8,128)(2,1)S(1)} all-gather(bf16[1,4,2,96,128]{4,3,2,1,0:T(8,128)(2,1)S(1)} %bitcast.29), channel_id=1, replica_groups=mesh['zh'=2,'zl'=4,'x'=4,'c'=2,'w'=2,'y'=4] {'x'}, dimensions={0}, use_global_device_ids=true | all-gather | bytes 983040 | tf_op jit(solution)/shard_map/all_gather | solution.py:257
  190.3 1.9 collective-permute-start.6
  192.3 0.0 all-to-all-done.1.parts
  192.3 2.2 merge.1
  194.4 7.0 %all-to-all-start.2 = ((bf16[4,144,128]{2,1,0:T(8,128)(2,1)}), bf16[4,144,128]{2,1,0:T(8,128)(2,1)S(1)}, u32[]{:S(2)}, u32[]{:S(2)}) async-start(bf16[4,144,128]{2,1,0:T(8,128)(2,1)} %merge.1), calls=%async_computation.2 | async-start | bytes 294912 | tf_op jit(solution)/shard_map/all_to_all | solution.py:254
  201.5 0.0 copy-done.10
  201.5 0.0 copy-done.11
  201.5 13.8 %all-to-all-done.2.got = bf16[4,144,128]{2,1,0:T(8,128)(2,1)S(1)} async-done(((bf16[4,144,128]{2,1,0:T(8,128)(2,1)}), bf16[4,144,128]{2,1,0:T(8,128)(2,1)S(1)}, u32[]{:S(2)}, u32[]{:S(2)}) %all-to-all-start.2) | async-done | bytes 147488 | tf_op jit(solution)/shard_map/all_to_all | solution.py:254
  215.3 13.8 %all-gather.3 = bf16[16,128,128]{2,1,0:T(8,128)(2,1)S(1)} all-gather(bf16[4,128,128]{2,1,0:T(8,128)(2,1)S(1)} %slice.42), channel_id=5, replica_groups=mesh['zh'=2,'zl'=4,'x'=4,'c'=2,'w'=2,'y'=4] {'y'}, dimensions={0}, use_global_device_ids=true | all-gather | bytes 655360 | tf_op jit(solution)/shard_map/all_gather | solution.py:255
  229.1 0.0 collective-permute-done.6.ooth
  229.1 1.8 finish.1
  (18 shorter events, 0.2 us)
Async XLA Ops:
  0.7 0.9 copy-start
  1.6 0.9 copy-start.1
  2.5 0.9 copy-start.2
  3.4 0.7 copy-start.3
  4.1 0.7 copy-start.4
  4.8 0.7 copy-start.5
  6.1 46.5 %collective-permute-start.3 = (bf16[400,128]{1,0:T(8,128)(2,1)S(1)}, bf16[400,128]{1,0:T(8,128)(2,1)S(1)}, u32[]{:S(2)}, u32[]{:S(2)}) collective-permute-start(bf16[400,128]{1,0:T(8,128)(2,1)S(1)} %get-tuple-element.9), channel_id=1, source_target_pairs={{0,256},{256,0},{1,257},{257,1},{2,258},{258,2},{3,259},{259,3},{4... | collective-permute-start | bytes 307208 | tf_op jit(solution)/shard_map/ppermute | solution.py:199
  81.1 26.7 %copy-start.9 = (f32[768]{0:T(1024)S(1)}, f32[768]{0:T(1024)}, u32[]{:S(2)}) copy-start(f32[768]{0:T(1024)} %param.14) | copy-start | bytes 9220
  81.1 40.8 %copy-start.6 = (f32[128]{0:T(128)S(1)}, f32[128]{0:T(128)}, u32[]{:S(2)}) copy-start(f32[128]{0:T(128)} %param.15) | copy-start | bytes 1540
  81.2 40.8 %copy-start.7 = (f32[128]{0:T(128)S(1)}, f32[128]{0:T(128)}, u32[]{:S(2)}) copy-start(f32[128]{0:T(128)} %param.16) | copy-start | bytes 1540
  94.3 27.6 %collective-permute-start.4 = (bf16[4,4,2,144,128]{4,3,2,1,0:T(8,128)(2,1)S(1)}, bf16[4,4,2,144,128]{4,3,2,1,0:T(8,128)(2,1)S(1)}, u32[]{:S(2)}, u32[]{:S(2)}) collective-permute-start(bf16[4,4,2,144,128]{4,3,2,1,0:T(8,128)(2,1)S(1)} %constant_dynamic-update-slice_fusion.wown), channel_id=1, source_target_pairs={{0,8},{8,0},{1,9},{9,1},{2,10},{10,2},{3,11},{11,3},{4,12},{12,4},... | collective-permute-start | bytes 3538952 | tf_op jit(solution)/shard_map/ppermute | solution.py:199
  96.3 14.7 %collective-permute-start = (bf16[4,384,128]{2,1,0:T(8,128)(2,1)S(1)}, bf16[4,384,128]{2,1,0:T(8,128)(2,1)S(1)}, u32[]{:S(2)}, u32[]{:S(2)}) collective-permute-start(bf16[4,384,128]{2,1,0:T(8,128)(2,1)S(1)} %slice.37.x0), channel_id=1, source_target_pairs={{0,1},{1,2},{2,3},{3,0},{4,5},{5,6},{6,7},{7,4},{8,9},{9,10},{10,1... | collective-permute-start | bytes 1179656 | tf_op jit(solution)/shard_map/ppermute | solution.py:203
  99.8 20.8 %collective-permute-start.1 = (bf16[4,384,128]{2,1,0:T(8,128)(2,1)S(1)}, bf16[4,384,128]{2,1,0:T(8,128)(2,1)S(1)}, u32[]{:S(2)}, u32[]{:S(2)}) collective-permute-start(bf16[4,384,128]{2,1,0:T(8,128)(2,1)S(1)} %slice.37.x0), channel_id=1, source_target_pairs={{0,2},{1,3},{2,0},{3,1},{4,6},{5,7},{6,4},{7,5},{8,10},{9,11},{10,... | collective-permute-start | bytes 1179656 | tf_op jit(solution)/shard_map/ppermute | solution.py:203
  104.6 17.3 %collective-permute-start.2 = (bf16[4,384,128]{2,1,0:T(8,128)(2,1)S(1)}, bf16[4,384,128]{2,1,0:T(8,128)(2,1)S(1)}, u32[]{:S(2)}, u32[]{:S(2)}) collective-permute-start(bf16[4,384,128]{2,1,0:T(8,128)(2,1)S(1)} %slice.37.x0), channel_id=1, source_target_pairs={{0,3},{1,0},{2,1},{3,2},{4,7},{5,4},{6,5},{7,6},{8,11},{9,8},{10,9... | collective-permute-start | bytes 1179656 | tf_op jit(solution)/shard_map/ppermute | solution.py:203
  123.7 23.2 %copy-start.8 = (s32[128,128]{1,0:T(8,128)S(1)}, s32[128,128]{1,0:T(8,128)}, u32[]{:S(2)}) copy-start(s32[128,128]{1,0:T(8,128)} %param.20) | copy-start | bytes 196612
  139.8 22.4 %collective-permute-start.5 = (bf16[4,512,128]{2,1,0:T(8,128)(2,1)S(1)}, bf16[4,512,128]{2,1,0:T(8,128)(2,1)S(1)}, u32[]{:S(2)}, u32[]{:S(2)}) collective-permute-start(bf16[4,512,128]{2,1,0:T(8,128)(2,1)S(1)} %bitcast.19), channel_id=1, source_target_pairs={{0,8},{8,0},{1,9},{9,1},{2,10},{10,2},{3,11},{11,3},{4,12},{12,4},... | collective-permute-start | bytes 1572872 | tf_op jit(solution)/shard_map/ppermute | solution.py:199
  142.4 14.3 %all-to-all-start = ((bf16[4,256,128]{2,1,0:T(8,128)(2,1)}), bf16[4,256,128]{2,1,0:T(8,128)(2,1)S(1)}, u32[]{:S(2)}, u32[]{:S(2)}) async-start(bf16[4,256,128]{2,1,0:T(8,128)(2,1)} %broadcast_in_dim.27), calls=%async_computation | async-start | bytes 524288 | tf_op jit(solution)/shard_map/all_to_all | solution.py:238
  156.8 10.7 %all-to-all-start.3 = ((bf16[4,192,128]{2,1,0:T(8,128)(2,1)}), bf16[4,192,128]{2,1,0:T(8,128)(2,1)S(1)}, u32[]{:S(2)}, u32[]{:S(2)}) async-start(bf16[4,192,128]{2,1,0:T(8,128)(2,1)} %slice.43), calls=%async_computation.3 | async-start | bytes 393216 | tf_op jit(solution)/shard_map/all_to_all | solution.py:230
  167.5 24.8 %all-to-all-start.1 = ((f32[4,168,256]{2,1,0:T(8,128)}), f32[4,168,256]{2,1,0:T(8,128)S(1)}, u32[]{:S(2)}, u32[]{:S(2)}) async-start(f32[4,168,256]{2,1,0:T(8,128)} %attend.1), calls=%async_computation.1 | async-start | bytes 1376256 | tf_op jit(solution)/shard_map/all_to_all | solution.py:252
  172.3 29.2 %copy-start.10 = (f32[384]{0:T(512)S(1)}, f32[384]{0:T(512)}, u32[]{:S(2)}) copy-start(f32[384]{0:T(512)} %param.22) | copy-start | bytes 4612
  172.3 29.2 %copy-start.11 = (f32[384]{0:T(512)S(1)}, f32[384]{0:T(512)}, u32[]{:S(2)}) copy-start(f32[384]{0:T(512)} %param.23) | copy-start | bytes 4612
  190.3 38.8 %collective-permute-start.6 = (bf16[4,4,2,96,128]{4,3,2,1,0:T(8,128)(2,1)S(1)}, bf16[4,4,2,96,128]{4,3,2,1,0:T(8,128)(2,1)S(1)}, u32[]{:S(2)}, u32[]{:S(2)}) collective-permute-start(bf16[4,4,2,96,128]{4,3,2,1,0:T(8,128)(2,1)S(1)} %all_gather.51.oown), channel_id=1, source_target_pairs={{0,8},{8,0},{1,9},{9,1},{2,10},{10,2},{3,11},{11,3},{4,12},{12,4},... | collective-permute-start | bytes 2359304 | tf_op jit(solution)/shard_map/ppermute | solution.py:199
  194.4 20.9 %all-to-all-start.2 = ((bf16[4,144,128]{2,1,0:T(8,128)(2,1)}), bf16[4,144,128]{2,1,0:T(8,128)(2,1)S(1)}, u32[]{:S(2)}, u32[]{:S(2)}) async-start(bf16[4,144,128]{2,1,0:T(8,128)(2,1)} %merge.1), calls=%async_computation.2 | async-start | bytes 294912 | tf_op jit(solution)/shard_map/all_to_all | solution.py:254

commit v2 on v1

v2 whole, which is shorter than its diff:
```python
import functools
import math

import jax
import jax.numpy as jnp
from jax import lax
from jax.experimental import pallas as pl
from jax.experimental.pallas import tpu as pltpu
from jax.sharding import Mesh, PartitionSpec as P

BF = jnp.bfloat16
F32 = jnp.float32
DH = 128
FRESH = 1e30
FLOOR = -1e29
SHUT = -1e30
LOG2E = 1.4426950408889634

VM = pl.BlockSpec(memory_space=pltpu.VMEM)
HB = pl.BlockSpec(memory_space=pltpu.HBM)


def call(kernel, outs, n_in, scratch=(), place=VM, limit=48, name=None, cover=0):
    multiple = isinstance(outs, (list, tuple))
    cost = pl.CostEstimate(flops=cover * 10**9, bytes_accessed=0, transcendentals=0) if cover else None
    return pl.pallas_call(
        kernel,
        out_shape=outs,
        in_specs=[place] * n_in,
        out_specs=[VM] * len(outs) if multiple else VM,
        scratch_shapes=list(scratch),
        compiler_params=pltpu.CompilerParams(vmem_limit_bytes=limit * 1024 * 1024 if limit else None),
        cost_estimate=cost,
        name=name,
    )


def nt(a, b, precision=None):
    return lax.dot_general(
        a, b, (((1,), (1,)), ((), ())), preferred_element_type=F32, precision=precision
    )


def tn(a, b):
    return lax.dot_general(a, b, (((0,), (0,)), ((), ())), preferred_element_type=F32)


def prep_kernel(
    scale_h, code_h, w_h, cache_h, tok_h, ot_h, keep_ref, send_ref, kept_ref, sent_ref, first_ref, flip_ref, scale, code,
    w_ref, cache_ref, tok_ref, ot_ref, sems
):
    zh = lax.axis_index("zh")
    pairs = ((w_h, w_ref), (cache_h, cache_ref), (scale_h, scale), (code_h, code), (tok_h, tok_ref), (ot_h, ot_ref))
    copies = [pltpu.make_async_copy(src, dst, sems.at[i]) for i, (src, dst) in enumerate(pairs)]
    for copy in copies:
        copy.start()
    for copy in copies:
        copy.wait()
    for t in range(3):
        a = w_ref[:, t * 128 : (t + 1) * 128]
        b = w_ref[:, 384 + t * 128 : 384 + (t + 1) * 128]
        keep_ref[t * 48 : (t + 1) * 48, :] = jnp.where(zh == 0, a, b)
        send_ref[t * 48 : (t + 1) * 48, :] = jnp.where(zh == 0, b, a)
    for part in range(2):
        for blk in range(2):
            rows = slice(blk * 64, blk * 64 + 64)
            at = slice(part * 128 + blk * 64, part * 128 + blk * 64 + 64)
            cached = jnp.broadcast_to(code[0:1, blk : blk + 1], (64, 128)) == 1
            both = []
            for j in range(2):
                raw = cache_ref[rows, j * 256 + part * 128 : j * 256 + part * 128 + 128]
                factor = jnp.broadcast_to(scale[blk : blk + 1, j : j + 1], (64, 128))
                both.append(jnp.where(cached, raw.astype(F32) * factor, FRESH).astype(BF))
            kept_ref[at, :] = jnp.where(zh == 0, both[0], both[1])
            sent_ref[at, :] = jnp.where(zh == 0, both[1], both[0])
    for f in range(3):
        first_ref[f * 128 : (f + 1) * 128, :] = tok_ref[:, f * 128 : (f + 1) * 128]
    for j in range(2):
        flip_ref[j * 48 : (j + 1) * 48, :] = ot_ref[:, j * 128 : (j + 1) * 128]


def projected(xa, xb, wown, woth):
    zh, c = lax.axis_index("zh"), lax.axis_index("c")
    total = jnp.zeros((256, 384), F32)
    for yy in range(4):
        for w in range(2):
            slot = jnp.where(zh == 0, w, 1 - w)
            rows = []
            for z in range(2):
                rows.append(jnp.concatenate([(xa, xb)[w][yy, z, f * 128 : (f + 1) * 128, :] for f in range(3)], axis=1))
            x = jnp.concatenate(rows, axis=0)
            pieces = []
            for xx in range(4):
                own = jnp.concatenate([wown[xx, yy, slot, t * 48 : (t + 1) * 48, :] for t in range(3)], axis=1)
                oth = jnp.concatenate([woth[xx, yy, slot, t * 48 : (t + 1) * 48, :] for t in range(3)], axis=1)
                pieces.append(jnp.where(c == 0, own, oth))
                pieces.append(jnp.where(c == 0, oth, own))
            total = total + jnp.dot(x, jnp.concatenate(pieces, axis=0), preferred_element_type=F32)
    return total


def scaled(v, gain):
    ms = jnp.mean(v * v, axis=-1, keepdims=True)
    return (v * lax.rsqrt(ms + 1e-06) * gain).astype(BF)


def project_kernel(xa, xb, wown, woth, bias, qg, kg, mine, theirs, out_ref, kv_ref):
    zh = lax.axis_index("zh")
    total = projected(xa, xb, wown, woth) + jnp.where(zh == 0, bias[:, :384], bias[:, 384:])
    q = scaled(total[:, :128], qg[...])
    for i in range(4):
        out_ref[i, :256, :] = q
        for z in range(4):
            out_ref[i, 256 + z * 192 : 352 + z * 192, :] = mine[z * 96 : (z + 1) * 96, :]
            out_ref[i, 352 + z * 192 : 448 + z * 192, :] = theirs[z * 96 : (z + 1) * 96, :]
    kv_ref[:256, :] = scaled(total[:, 128:256], kg[...])
    kv_ref[256:, :] = total[:, 256:].astype(BF)


def select_kernel(fresh, kept, theirs, kv_ref):
    zh = lax.axis_index("zh")
    for part in range(2):
        a = kept[part * 128 : part * 128 + 128, :]
        b = theirs[384 + part * 128 : 384 + part * 128 + 128, :]
        for z in range(2):
            rows = slice(part * 256 + z * 128, part * 256 + (z + 1) * 128)
            cached = jnp.where(zh == z, a, b)
            kv_ref[rows, :] = jnp.where(cached.astype(F32) < 1e29, cached, fresh[rows, :])


def attend_kernel(q_ref, kv0, kv1, bm_ref, out_ref, s_ref, mask_ref):
    unit = LOG2E / math.sqrt(DH)
    zl, x, c = (lax.axis_index(n) for n in ("zl", "x", "c"))
    r = lax.broadcasted_iota(jnp.int32, (32, 128), 0)
    b = lax.broadcasted_iota(jnp.int32, (32, 128), 1)
    cc = jnp.bitwise_xor(r >> 4, c)
    keys = ((r >> 1) & 1) * 64 + ((r >> 2) & 3) * 16 + x * 4 + cc * 2 + (r & 1)
    picked = nt((keys == b).astype(BF), bm_ref[...].astype(F32).astype(BF))
    a = lax.broadcasted_iota(jnp.int32, (128, 1024), 0)
    t = lax.broadcasted_iota(jnp.int32, (128, 1024), 1)
    rows = ((t >> 7) & 1) * 64 + zl * 16 + (t >> 8) * 4 + c * 2 + ((t >> 6) & 1)
    mask_ref[...] = jnp.dot(picked.astype(BF), (rows == a).astype(BF), preferred_element_type=F32)
    q = jnp.concatenate([q_ref[i, :256, :] for i in range(4)], axis=0)
    top = jnp.full((1, 1024), FLOOR, F32)
    for ch in range(8):
        kv = (kv0, kv1)[ch // 4]
        s = nt(kv[ch % 4, :256, :], q) * unit
        for b in range(4):
            row = ch * 4 + b
            open_ = mask_ref[row : row + 1, :] > 0.5
            sb = jnp.where(open_, s[b * 64 : (b + 1) * 64], SHUT)
            s_ref[ch * 256 + b * 64 : ch * 256 + (b + 1) * 64, :] = sb
            top = jnp.maximum(top, jnp.max(sb, axis=0, keepdims=True))
    total = jnp.zeros((1, 1024), F32)
    out = jnp.zeros((128, 1024), F32)
    mass = []
    for ch in range(8):
        kv = (kv0, kv1)[ch // 4]
        p = jnp.exp2(s_ref[ch * 256 : (ch + 1) * 256, :] - top)
        for b in range(4):
            row = jnp.sum(p[b * 64 : (b + 1) * 64], axis=0, keepdims=True)
            mass.append(row)
            total = total + row
        out = out + tn(kv[ch % 4, 256:, :], p.astype(BF))
    for i in range(4):
        cols = slice(i * 256, (i + 1) * 256)
        out_ref[i, :128, :] = out[:, cols]
        for r in range(32):
            out_ref[i, 128 + r : 129 + r, :] = mass[r][:, cols]
        out_ref[i, 160:161, :] = top[:, cols]
        out_ref[i, 161:162, :] = total[:, cols]
        out_ref[i, 162:168, :] = jnp.zeros((6, 256), F32)


def merge_kernel(parts, out_ref):
    c = lax.axis_index("c")
    hi = lax.Precision.HIGHEST
    tops = [parts[i, 160:161, :] for i in range(4)]
    top = jnp.maximum(jnp.maximum(tops[0], tops[1]), jnp.maximum(tops[2], tops[3]))
    factors = [jnp.exp2(t - top) for t in tops]
    total = sum(f * parts[i, 161:162, :] for i, f in enumerate(factors))
    shares = [f / total for f in factors]
    out = sum(s * parts[i, :128, :] for i, s in enumerate(shares))
    att = out.T.astype(BF)
    mass = jnp.concatenate([s * parts[i, 128:160, :] for i, s in enumerate(shares)], axis=0)
    i = lax.broadcasted_iota(jnp.int32, (128, 128), 0)
    b = lax.broadcasted_iota(jnp.int32, (128, 128), 1)
    cc = jnp.bitwise_xor((i >> 4) & 1, c)
    place = ((i >> 1) & 1) * 64 + ((i >> 2) & 3) * 16 + (i >> 5) * 4 + cc * 2 + (i & 1)
    order = (place == b).astype(F32)
    r = lax.broadcasted_iota(jnp.int32, (16, 256), 0)
    t = lax.broadcasted_iota(jnp.int32, (16, 256), 1)
    row = lax.broadcasted_iota(jnp.int32, (16, 128), 0)
    pick = ((r < 12) & ((t >> 6) == (r & 3))).astype(F32)
    m = jnp.dot(nt(pick, mass, hi), order, preferred_element_type=F32, precision=hi)
    a = m.astype(BF).astype(F32)
    d = (m - a).astype(BF).astype(F32)
    e = m - a - d
    packed = jnp.where(row < 4, a, jnp.where(row < 8, d, jnp.where(row < 12, e, 0.0))).astype(BF)
    out_ref[:256, :] = att
    out_ref[256:272, :] = packed


def finish_kernel(att, rows, oown, ooth, bias, gate, out_ref, mass_ref):
    zh, c, w = (lax.axis_index(n) for n in ("zh", "c", "w"))
    a = jnp.concatenate([att[y, i] for y in range(4) for i in range(4)], axis=1)
    weights = []
    for x in range(4):
        both = []
        for ref in (oown, ooth):
            piece = []
            for y in range(4):
                for ww in range(2):
                    slot = jnp.where(zh == 0, ww, 1 - ww)
                    for j in range(2):
                        start = pl.multiple_of(256 + y * 192 + slot * 96 + j * 48, 16)
                        piece.append(ref[x, pl.ds(start, 48), :])
            both.append(jnp.concatenate(piece, axis=1))
        weights.append(jnp.where(c == 0, both[0], both[1]))
        weights.append(jnp.where(c == 0, both[1], both[0]))
    total = nt(a, jnp.concatenate(weights, axis=0))
    out_ref[...] = ((total + bias[...]) * gate[...]).astype(BF)
    for j in range(2):
        r = rows[w * 2 + j, 256:272, :].astype(F32)
        lower = r[0:2] + r[4:6] + r[8:10]
        upper = r[2:4] + r[6:8] + r[10:12]
        mass_ref[j] = jnp.where(zh == 0, lower, upper)


def swap(v, axis):
    return lax.ppermute(v, axis, [(0, 1), (1, 0)])


def spread(v, axis):
    wide = jnp.broadcast_to(v[None], (4,) + v.shape)
    return lax.all_to_all(wide, axis, 0, 0, tiled=True)


def turn(v, axis, k):
    return lax.ppermute(v, axis, [(i, (i + k) % 4) for i in range(4)])


def per_device(
    tokens, qkv_weight, qkv_bias, q_gain, k_gain, cache_kv, cache_scale, cache_code, block_mask, out_weight,
    out_bias, out_gate,
):
    sd = jax.ShapeDtypeStruct

    keep, send, kept, sent, first, flip = call(
        prep_kernel,
        [sd((144, 128), BF)] * 2 + [sd((256, 128), BF)] * 2 + [sd((384, 128), BF), sd((96, 128), BF)],
        6,
        [
            pltpu.VMEM((2, 2), F32), pltpu.VMEM((1, 2), jnp.int32), pltpu.VMEM((48, 768), BF),
            pltpu.VMEM((128, 512), BF), pltpu.VMEM((128, 384), BF), pltpu.VMEM((48, 256), BF),
            pltpu.SemaphoreType.DMA((6,)),
        ],
        HB, None, "prep",
    )(cache_scale, cache_code.reshape(1, 2), qkv_weight, cache_kv, tokens, out_weight.T)

    recv = swap(send, "zh")
    flip = lax.ppermute(
        flip, ("zh", "zl", "w", "y"),
        [
            (((zh * 4 + zl) * 2 + w) * 4 + y, ((w * 4 + y) * 2 + zh) * 4 + zl)
            for zh in range(2) for zl in range(4) for w in range(2) for y in range(4)
        ],
    )
    pay, first = lax.optimization_barrier((jnp.concatenate([keep, recv, flip], axis=0), first))
    along = spread(pay, "zl").reshape(4, 384, 128)
    toks = lax.all_gather(first, ("w", "zh"), axis=0, tiled=False)
    along, toks = lax.optimization_barrier((along, toks))
    wown = spread(along[:, :288], "x")
    xa = lax.all_gather(toks[:2], "y", axis=0, tiled=False)
    wown, xa, last = lax.optimization_barrier((wown, xa, toks[2:]))
    woth = swap(wown, "c")
    mine = jnp.concatenate([along[:, 288:].reshape(384, 128), sent], axis=0)
    theirs = swap(mine, "zh")
    xb = lax.all_gather(last, "y", axis=0, tiled=False)
    woth, theirs, xb = lax.optimization_barrier((woth, theirs, xb))
    woth = woth.reshape(4, 4, 2, 144, 128)
    wown = wown.reshape(4, 4, 2, 144, 128)

    q, fresh = call(project_kernel, [sd((4, 1024, 128), BF), sd((512, 128), BF)], 9, limit=24, name="project")(
        xa, xb, wown, woth, qkv_bias[None], q_gain[None], k_gain[None], mine, theirs
    )
    qs = lax.all_to_all(q, "x", 0, 0, tiled=True)
    kv = call(select_kernel, sd((512, 128), BF), 3, limit=24, name="select", cover=30)(fresh, kept, theirs)
    kv0 = lax.all_gather(kv, "zl", axis=0, tiled=False)
    kv1 = swap(kv0, "c")

    parts = call(
        attend_kernel, sd((4, 168, 256), F32), 4, [pltpu.VMEM((2048, 1024), F32), pltpu.VMEM((32, 1024), F32)],
        limit=32, name="attend",
    )(qs, kv0, kv1, block_mask)
    late, parts = lax.optimization_barrier((qs, parts))
    parts = lax.all_to_all(parts, "x", 0, 0, tiled=True)
    ooth = swap(late, "c")
    parts, ooth = lax.optimization_barrier((parts, ooth))
    done = call(merge_kernel, sd((272, 128), BF), 1, limit=16, name="merge")(parts)
    rows = lax.all_gather(done, ("w", "zh"), axis=0, tiled=False)
    att = lax.all_gather(
        lax.dynamic_slice_in_dim(rows, lax.axis_index("zh") * 128, 128, 1), "y", axis=0, tiled=False
    )
    return call(finish_kernel, [sd((128, 384), BF), sd((2, 2, 128), F32)], 6, limit=24, name="finish")(
        att, rows, qs, ooth, out_bias[None], out_gate[None]
    )


def solution(mesh):
    split = Mesh(mesh.devices.reshape(2, 4, 4, 2, 2, 4), ("zh", "zl", "x", "c", "w", "y"))
    seq, head = ("zh", "zl", "x", "c"), ("w", "y")
    in_specs = (
        P(seq, head), P(seq, head), P(head), P(), P(), P(seq, head), P(seq, head), P(seq), P(), P(head, seq),
        P(head), P(head),
    )
    out_specs = (P(seq, head), P(head, seq, None))
    return jax.shard_map(per_device, mesh=split, in_specs=in_specs, out_specs=out_specs, check_vma=False)
```

time: 234 us -> 189 us (0.81)
  blocking collectives: 127 us -> 110 us
  waiting for transfers between devices: 28.3 us -> 12.3 us
  local copies, waits for them, and re-layouts: 16.5 us -> 2.1 us
  starting transfers between devices: 47.1 us -> 49.8 us
    all_gather x6 -> x5, blocking collectives: 111 us -> 89.7 us  [the longest x1 28.5 us: per_device(): toks = lax.all_gather(first, ('w', 'zh'), axis=0, tiled=False)]
    all_to_all x3, waiting for transfers between devices: 14.3 us -> 0.01 us  [the longest x2 0.01 us: spread(): return lax.all_to_all(wide, axis, 0, 0, tiled=True)]
    ppermute x3 -> x1, waiting for transfers between devices: 14.1 us -> 0.01 us  [per_device(): lax.ppermute(flip, ('zh', 'zl', 'w', 'y'), [(((zh * 4 + zl) * 2 + w) * 4...]
    ppermute x3 -> x1, starting transfers between devices: 11.6 us -> 1.4 us  [per_device(): lax.ppermute(flip, ('zh', 'zl', 'w', 'y'), [(((zh * 4 + zl) * 2 + w) * 4...]
    all_to_all x1, waiting for transfers between devices: 0.01 us -> 9.67 us  [per_device(): parts = lax.all_to_all(parts, 'x', 0, 0, tiled=True)]
    reshape x2 -> x0, local copies, waits for them, and re-layouts: 7.85 us -> none  [the longest x1 7.72 us: per_device(): bm = block_mask.reshape(2, 4, 4, 2, 2, 2, 4, 4, 2, 2)]
    all_to_all x3, starting transfers between devices: 15.9 us -> 23.3 us  [the longest x2 18.4 us: spread(): return lax.all_to_all(wide, axis, 0, 0, tiled=True)]
    ppermute x4 -> x5, starting transfers between devices: 14.8 us -> 20.2 us  [swap(): return lax.ppermute(v, axis, [(0, 1), (1, 0)])]
  transfers between devices with their start and end apart: 11 -> 10, of which waited for: 5 -> 3; matrix products, arithmetic and copies ran while one was open for 5% -> 0% of each run, Pallas kernels for 3% -> 0%
where the time goes in v2:
time: 189 us; the launch traced here: 187 us
  blocking collectives  110 us (58%)
  starting transfers between devices  49.8 us (26%)
  waiting for transfers between devices  12.3 us (7%)
  Pallas kernels  10.8 us (6%)
  local copies, waits for them, and re-layouts  2.1 us (1%)
    all_gather x1, blocking collectives, per_device(): toks = lax.all_gather(first, ('w', 'zh'), axis=0, tiled=False)  28.5 us
    all_gather x1, blocking collectives, per_device(): kv0 = lax.all_gather(kv, 'zl', axis=0, tiled=False)  20.7 us
    ppermute x5, starting transfers between devices, swap(): return lax.ppermute(v, axis, [(0, 1), (1, 0)])  20.2 us
    all_gather x1, blocking collectives, per_device(): rows = lax.all_gather(done, ('w', 'zh'), axis=0, tiled=False)  20.2 us
    all_to_all x2, starting transfers between devices, spread(): return lax.all_to_all(wide, axis, 0, 0, tiled=True)  18.4 us
    all_gather x1, blocking collectives, per_device(): xb = lax.all_gather(last, 'y', axis=0, tiled=False)  14.5 us
    all_gather x1, blocking collectives, per_device(): xa = lax.all_gather(toks[:2], 'y', axis=0, tiled=False)  13.4 us
    all_gather x1, blocking collectives, per_device(): lax.all_gather(lax.dynamic_slice_in_dim(rows, lax.axis_index('zh') * 128,...  13 us
  transfers between devices with their start and end apart: 10, of which 3 were waited for; matrix products, arithmetic and copies ran while one was open for 0% of the time, Pallas kernels for 0%

profile of v2, /device:TPU:6, one launch (start us, length us, event | category | flops | bytes accessed | tf_op | source)
XLA Modules:
  0.0 187.0 jit_solution(17534293286247379567)
XLA Ops:
  0.6 1.9 %prep.1 = (bf16[144,128]{1,0:T(8,128)(2,1)}, bf16[144,128]{1,0:T(8,128)(2,1)}, bf16[256,128]{1,0:T(8,128)(2,1)}, bf16[256,128]{1,0:T(8,128)(2,1)}, bf16[384,128]{1,0:T(8,128)(2,1)}, /*index=5*/bf16[96,128]{1,0:T(8,128)(2,1)}) custom-call(f32[2,2]{1,0:T(2,128)} %scale_h.1, s32[1,2]{1,0:T(1,128)} %bitcast.27, bf16[48,768]{1,0:T(8,128)(2,1)} %w_h.1, ...), custom_call_target="tpu_custom_call" | custom-call | tf_op jit(solution)/shard_map/prep/pallas_call | solution.py:249
  2.5 0.0 copy-start.4
  2.6 9.2 %collective-permute-start = (bf16[144,128]{1,0:T(8,128)(2,1)}, bf16[144,128]{1,0:T(8,128)(2,1)S(1)}, u32[]{:S(2)}, u32[]{:S(2)}) collective-permute-start(bf16[144,128]{1,0:T(8,128)(2,1)} %get-tuple-element.25), channel_id=1, source_target_pairs={{0,256},{256,0},{1,257},{257,1},{2,258},{258,2},{3,259},{259,3},{4... | collective-permute-start | bytes 110600 | tf_op jit(solution)/shard_map/ppermute | solution.py:231
  11.8 1.4 collective-permute-start.1
  13.2 0.0 collective-permute-done.1
  13.2 0.7 collective-permute-done
  13.9 0.8 pad_maximum_fusion.1
  14.7 0.8 broadcast_in_dim.27
  15.5 13.6 %all-to-all-start = ((bf16[4,384,128]{2,1,0:T(8,128)(2,1)}), bf16[4,384,128]{2,1,0:T(8,128)(2,1)S(1)}, u32[]{:S(2)}, u32[]{:S(2)}) async-start(bf16[4,384,128]{2,1,0:T(8,128)(2,1)} %broadcast_in_dim.27), calls=%async_computation | async-start | bytes 786432 | tf_op jit(solution)/shard_map/all_to_all | solution.py:236
  29.1 0.0 copy-done.4
  29.1 28.5 %all-gather = bf16[1536,128]{1,0:T(8,128)(2,1)S(1)} all-gather(bf16[384,128]{1,0:T(8,128)(2,1)S(1)} %copy-done.4), channel_id=2, replica_groups=mesh['zh'=2,'zl'=4,'x'=4,'c'=2,'w'=2,'y'=4] {'w','zh'}, dimensions={0}, use_global_device_ids=true | all-gather | bytes 491520 | tf_op jit(solution)/shard_map/all_gather | solution.py:271
  57.6 0.0 all-to-all-done
  57.7 1.2 broadcast_in_dim.28
  58.8 4.8 %all-to-all-start.1 = ((bf16[4,4,288,128]{3,2,1,0:T(8,128)(2,1)}), bf16[4,4,288,128]{3,2,1,0:T(8,128)(2,1)S(1)}, u32[]{:S(2)}, u32[]{:S(2)}) async-start(bf16[4,4,288,128]{3,2,1,0:T(8,128)(2,1)} %broadcast_in_dim.28), calls=%async_computation.1 | async-start | bytes 2359296 | tf_op jit(solution)/shard_map/all_to_all | solution.py:236
  63.6 0.0 copy-start.6
  63.6 0.0 copy-start.5
  63.6 0.0 copy-start.1
  63.7 0.0 copy-start.2
  63.7 13.4 %all-gather.1 = bf16[8,384,128]{2,1,0:T(8,128)(2,1)S(1)} all-gather(bf16[2,384,128]{2,1,0:T(8,128)(2,1)S(1)} %get-tuple-element.47), channel_id=3, replica_groups=mesh['zh'=2,'zl'=4,'x'=4,'c'=2,'w'=2,'y'=4] {'y'}, dimensions={0}, use_global_device_ids=true | all-gather | bytes 983040 | tf_op jit(solution)/shard_map/all_gather | solution.py:274
  77.1 0.0 all-to-all-done.1
  77.1 1.9 %collective-permute-start.2 = (bf16[4,4,288,128]{3,2,1,0:T(8,128)(2,1)S(1)}, bf16[4,4,288,128]{3,2,1,0:T(8,128)(2,1)S(1)}, u32[]{:S(2)}, u32[]{:S(2)}) collective-permute-start(bf16[4,4,288,128]{3,2,1,0:T(8,128)(2,1)S(1)} %all-to-all-done.1), channel_id=1, source_target_pairs={{0,8},{8,0},{1,9},{9,1},{2,10},{10,2},{3,11},{11,3},{4,12},{12,4},... | collective-permute-start | bytes 3538952 | tf_op jit(solution)/shard_map/ppermute | solution.py:231
  79.0 0.0 copy-done.6
  79.1 0.0 copy-done.5
  79.1 5.0 %collective-permute-start.3 = (bf16[640,128]{1,0:T(8,128)(2,1)S(1)}, bf16[640,128]{1,0:T(8,128)(2,1)S(1)}, u32[]{:S(2)}, u32[]{:S(2)}) collective-permute-start(bf16[640,128]{1,0:T(8,128)(2,1)S(1)} %pad_maximum_fusion.mine), channel_id=1, source_target_pairs={{0,256},{256,0},{1,257},{257,1},{2,258},{258,2},{3,259},{259,3},{4... | collective-permute-start | bytes 491528 | tf_op jit(solution)/shard_map/ppermute | solution.py:231
  84.2 14.5 %all-gather.2 = bf16[8,384,128]{2,1,0:T(8,128)(2,1)S(1)} all-gather(bf16[2,384,128]{2,1,0:T(8,128)(2,1)S(1)} %get-tuple-element.35), channel_id=4, replica_groups=mesh['zh'=2,'zl'=4,'x'=4,'c'=2,'w'=2,'y'=4] {'y'}, dimensions={0}, use_global_device_ids=true | all-gather | bytes 983040 | tf_op jit(solution)/shard_map/all_gather | solution.py:279
  98.7 0.0 collective-permute-done.3.theirs
  98.7 0.0 collective-permute-done.2
  98.7 0.0 copy-done.1
  98.7 0.0 copy-done.2
  98.7 2.3 %project.1 = (bf16[4,1024,128]{2,1,0:T(8,128)(2,1)}, bf16[512,128]{1,0:T(8,128)(2,1)S(1)}) custom-call(bf16[4,2,384,128]{3,2,1,0:T(8,128)(2,1)S(1)} %bitcast.14, bf16[4,2,384,128]{3,2,1,0:T(8,128)(2,1)S(1)} %bitcast.15, bf16[4,4,2,144,128]{4,3,2,1,0:T(8,128)(2,1)S(1)} %bitcast.13, bf16[4,4,2,144,128]{4,3,2,1,0:T(8,128)(2,1)S(1)} %bitcast.21, ...), custom_call_target="tpu_custom_call" | custom-call | tf_op jit(solution)/shard_map/project/pallas_call | solution.py:284
  101.0 0.0 copy-start.3
  101.0 4.9 %all-to-all-start.2 = ((bf16[4,1024,128]{2,1,0:T(8,128)(2,1)}), bf16[4,1024,128]{2,1,0:T(8,128)(2,1)S(1)}, u32[]{:S(2)}, u32[]{:S(2)}) async-start(bf16[4,1024,128]{2,1,0:T(8,128)(2,1)} %get-tuple-element.39), calls=%async_computation.2 | async-start | bytes 2097152 | tf_op jit(solution)/shard_map/all_to_all | solution.py:287
  105.9 0.0 copy-done.3
  105.9 0.0 copy-start
  105.9 0.1 select.1
  106.0 20.7 %all-gather.3 = bf16[2048,128]{1,0:T(8,128)(2,1)S(1)} all-gather(bf16[512,128]{1,0:T(8,128)(2,1)S(1)} %select.1), channel_id=5, replica_groups=mesh['zh'=2,'zl'=4,'x'=4,'c'=2,'w'=2,'y'=4] {'zl'}, dimensions={0}, use_global_device_ids=true | all-gather | bytes 655360 | tf_op jit(solution)/shard_map/all_gather | solution.py:289
  126.6 1.9 %collective-permute-start.4 = (bf16[4,512,128]{2,1,0:T(8,128)(2,1)S(1)}, bf16[4,512,128]{2,1,0:T(8,128)(2,1)S(1)}, u32[]{:S(2)}, u32[]{:S(2)}) collective-permute-start(bf16[4,512,128]{2,1,0:T(8,128)(2,1)S(1)} %bitcast.16), channel_id=1, source_target_pairs={{0,8},{8,0},{1,9},{9,1},{2,10},{10,2},{3,11},{11,3},{4,12},{12,4},... | collective-permute-start | bytes 1572872 | tf_op jit(solution)/shard_map/ppermute | solution.py:231
  128.5 1.9 %collective-permute-done.4.kv1 = bf16[4,512,128]{2,1,0:T(8,128)(2,1)S(1)} collective-permute-done((bf16[4,512,128]{2,1,0:T(8,128)(2,1)S(1)}, bf16[4,512,128]{2,1,0:T(8,128)(2,1)S(1)}, u32[]{:S(2)}, u32[]{:S(2)}) %collective-permute-start.4) | collective-permute-done | bytes 524320 | tf_op jit(solution)/shard_map/ppermute | solution.py:231
  130.4 0.0 all-to-all-done.2.q_ref.oown
  130.4 0.0 copy-done
  130.4 4.9 %attend.1 = f32[4,168,256]{2,1,0:T(8,128)} custom-call(bf16[4,1024,128]{2,1,0:T(8,128)(2,1)S(1)} %all-to-all-done.2.q_ref.oown, bf16[4,512,128]{2,1,0:T(8,128)(2,1)S(1)} %bitcast.17, bf16[4,512,128]{2,1,0:T(8,128)(2,1)S(1)} %collective-permute-done.4.kv1, s32[128,128]{1,0:T(8,128)S(1)} %copy-done), custom_call_target="tpu_custom_call" | custom-call | tf_op jit(solution)/shard_map/attend/pallas_call | solution.py:292
  135.3 0.0 copy-start.7
  135.3 0.0 copy-start.8
  135.3 2.2 %collective-permute-start.5 = (bf16[4,1024,128]{2,1,0:T(8,128)(2,1)S(1)}, bf16[4,1024,128]{2,1,0:T(8,128)(2,1)S(1)}, u32[]{:S(2)}, u32[]{:S(2)}) collective-permute-start(bf16[4,1024,128]{2,1,0:T(8,128)(2,1)S(1)} %all-to-all-done.2.q_ref.oown), channel_id=1, source_target_pairs={{0,8},{8,0},{1,9},{9,1},{2,10},{10,2},{3,11},{11,3},{4,12},{12,4},... | collective-permute-start | bytes 3145736 | tf_op jit(solution)/shard_map/ppermute | solution.py:231
  137.5 4.9 %all-to-all-start.3 = ((f32[4,168,256]{2,1,0:T(8,128)}), f32[4,168,256]{2,1,0:T(8,128)S(1)}, u32[]{:S(2)}, u32[]{:S(2)}) async-start(f32[4,168,256]{2,1,0:T(8,128)} %attend.1), calls=%async_computation.3 | async-start | bytes 1376256 | tf_op jit(solution)/shard_map/all_to_all | solution.py:297
  142.4 0.0 copy-done.7
  142.4 0.0 copy-done.8
  142.4 9.7 %all-to-all-done.3.parts = f32[4,168,256]{2,1,0:T(8,128)S(1)} async-done(((f32[4,168,256]{2,1,0:T(8,128)}), f32[4,168,256]{2,1,0:T(8,128)S(1)}, u32[]{:S(2)}, u32[]{:S(2)}) %all-to-all-start.3) | async-done | bytes 688160 | tf_op jit(solution)/shard_map/all_to_all | solution.py:297
  152.0 0.0 collective-permute-done.5.ooth
  152.1 0.5 merge.1
  152.5 20.2 %all-gather.4 = bf16[1088,128]{1,0:T(8,128)(2,1)S(1)} all-gather(bf16[272,128]{1,0:T(8,128)(2,1)S(1)} %merge.1), channel_id=6, replica_groups=mesh['zh'=2,'zl'=4,'x'=4,'c'=2,'w'=2,'y'=4] {'w','zh'}, dimensions={0}, use_global_device_ids=true | all-gather | bytes 348160 | tf_op jit(solution)/shard_map/all_gather | solution.py:301
  172.8 13.0 %all-gather.5 = bf16[16,128,128]{2,1,0:T(8,128)(2,1)S(1)} all-gather(bf16[4,128,128]{2,1,0:T(8,128)(2,1)S(1)} %constant_dynamic-slice_fusion), channel_id=7, replica_groups=mesh['zh'=2,'zl'=4,'x'=4,'c'=2,'w'=2,'y'=4] {'y'}, dimensions={0}, use_global_device_ids=true | all-gather | bytes 655360 | tf_op jit(solution)/shard_map/all_gather | solution.py:302
  185.8 1.3 finish.1
  (8 shorter events, 0.1 us)
Async XLA Ops:
  2.5 26.6 %copy-start.4 = (bf16[384,128]{1,0:T(8,128)(2,1)S(1)}, bf16[384,128]{1,0:T(8,128)(2,1)}, u32[]{:S(2)}) copy-start(bf16[384,128]{1,0:T(8,128)(2,1)} %get-tuple-element.29) | copy-start | bytes 294916
  2.6 11.4 %collective-permute-start = (bf16[144,128]{1,0:T(8,128)(2,1)}, bf16[144,128]{1,0:T(8,128)(2,1)S(1)}, u32[]{:S(2)}, u32[]{:S(2)}) collective-permute-start(bf16[144,128]{1,0:T(8,128)(2,1)} %get-tuple-element.25), channel_id=1, source_target_pairs={{0,256},{256,0},{1,257},{257,1},{2,258},{258,2},{3,259},{259,3},{4... | collective-permute-start | bytes 110600 | tf_op jit(solution)/shard_map/ppermute | solution.py:231
  11.8 1.4 collective-permute-start.1
  15.5 42.1 %all-to-all-start = ((bf16[4,384,128]{2,1,0:T(8,128)(2,1)}), bf16[4,384,128]{2,1,0:T(8,128)(2,1)S(1)}, u32[]{:S(2)}, u32[]{:S(2)}) async-start(bf16[4,384,128]{2,1,0:T(8,128)(2,1)} %broadcast_in_dim.27), calls=%async_computation | async-start | bytes 786432 | tf_op jit(solution)/shard_map/all_to_all | solution.py:236
  58.8 18.3 %all-to-all-start.1 = ((bf16[4,4,288,128]{3,2,1,0:T(8,128)(2,1)}), bf16[4,4,288,128]{3,2,1,0:T(8,128)(2,1)S(1)}, u32[]{:S(2)}, u32[]{:S(2)}) async-start(bf16[4,4,288,128]{3,2,1,0:T(8,128)(2,1)} %broadcast_in_dim.28), calls=%async_computation.1 | async-start | bytes 2359296 | tf_op jit(solution)/shard_map/all_to_all | solution.py:236
  63.6 15.4 %copy-start.6 = (f32[768]{0:T(1024)S(1)}, f32[768]{0:T(1024)}, u32[]{:S(2)}) copy-start(f32[768]{0:T(1024)} %param.14) | copy-start | bytes 9220
  63.6 15.5 %copy-start.5 = (bf16[256,128]{1,0:T(8,128)(2,1)S(1)}, bf16[256,128]{1,0:T(8,128)(2,1)}, u32[]{:S(2)}) copy-start(bf16[256,128]{1,0:T(8,128)(2,1)} %get-tuple-element.34) | copy-start | bytes 196612
  63.6 35.0 %copy-start.1 = (f32[128]{0:T(128)S(1)}, f32[128]{0:T(128)}, u32[]{:S(2)}) copy-start(f32[128]{0:T(128)} %param.15) | copy-start | bytes 1540
  63.7 35.0 %copy-start.2 = (f32[128]{0:T(128)S(1)}, f32[128]{0:T(128)}, u32[]{:S(2)}) copy-start(f32[128]{0:T(128)} %param.16) | copy-start | bytes 1540
  77.1 21.6 %collective-permute-start.2 = (bf16[4,4,288,128]{3,2,1,0:T(8,128)(2,1)S(1)}, bf16[4,4,288,128]{3,2,1,0:T(8,128)(2,1)S(1)}, u32[]{:S(2)}, u32[]{:S(2)}) collective-permute-start(bf16[4,4,288,128]{3,2,1,0:T(8,128)(2,1)S(1)} %all-to-all-done.1), channel_id=1, source_target_pairs={{0,8},{8,0},{1,9},{9,1},{2,10},{10,2},{3,11},{11,3},{4,12},{12,4},... | collective-permute-start | bytes 3538952 | tf_op jit(solution)/shard_map/ppermute | solution.py:231
  79.1 19.6 %collective-permute-start.3 = (bf16[640,128]{1,0:T(8,128)(2,1)S(1)}, bf16[640,128]{1,0:T(8,128)(2,1)S(1)}, u32[]{:S(2)}, u32[]{:S(2)}) collective-permute-start(bf16[640,128]{1,0:T(8,128)(2,1)S(1)} %pad_maximum_fusion.mine), channel_id=1, source_target_pairs={{0,256},{256,0},{1,257},{257,1},{2,258},{258,2},{3,259},{259,3},{4... | collective-permute-start | bytes 491528 | tf_op jit(solution)/shard_map/ppermute | solution.py:231
  101.0 4.9 %copy-start.3 = (bf16[256,128]{1,0:T(8,128)(2,1)S(1)}, bf16[256,128]{1,0:T(8,128)(2,1)}, u32[]{:S(2)}) copy-start(bf16[256,128]{1,0:T(8,128)(2,1)} %get-tuple-element.41.kept) | copy-start | bytes 196612
  101.0 29.5 %all-to-all-start.2 = ((bf16[4,1024,128]{2,1,0:T(8,128)(2,1)}), bf16[4,1024,128]{2,1,0:T(8,128)(2,1)S(1)}, u32[]{:S(2)}, u32[]{:S(2)}) async-start(bf16[4,1024,128]{2,1,0:T(8,128)(2,1)} %get-tuple-element.39), calls=%async_computation.2 | async-start | bytes 2097152 | tf_op jit(solution)/shard_map/all_to_all | solution.py:287
  105.9 24.5 %copy-start = (s32[128,128]{1,0:T(8,128)S(1)}, s32[128,128]{1,0:T(8,128)}, u32[]{:S(2)}) copy-start(s32[128,128]{1,0:T(8,128)} %bm_ref.1) | copy-start | bytes 196612
  126.6 3.8 %collective-permute-start.4 = (bf16[4,512,128]{2,1,0:T(8,128)(2,1)S(1)}, bf16[4,512,128]{2,1,0:T(8,128)(2,1)S(1)}, u32[]{:S(2)}, u32[]{:S(2)}) collective-permute-start(bf16[4,512,128]{2,1,0:T(8,128)(2,1)S(1)} %bitcast.16), channel_id=1, source_target_pairs={{0,8},{8,0},{1,9},{9,1},{2,10},{10,2},{3,11},{11,3},{4,12},{12,4},... | collective-permute-start | bytes 1572872 | tf_op jit(solution)/shard_map/ppermute | solution.py:231
  135.3 7.1 %copy-start.7 = (f32[384]{0:T(512)S(1)}, f32[384]{0:T(512)}, u32[]{:S(2)}) copy-start(f32[384]{0:T(512)} %param.22) | copy-start | bytes 4612
  135.3 7.1 %copy-start.8 = (f32[384]{0:T(512)S(1)}, f32[384]{0:T(512)}, u32[]{:S(2)}) copy-start(f32[384]{0:T(512)} %param.23) | copy-start | bytes 4612
  135.3 16.8 %collective-permute-start.5 = (bf16[4,1024,128]{2,1,0:T(8,128)(2,1)S(1)}, bf16[4,1024,128]{2,1,0:T(8,128)(2,1)S(1)}, u32[]{:S(2)}, u32[]{:S(2)}) collective-permute-start(bf16[4,1024,128]{2,1,0:T(8,128)(2,1)S(1)} %all-to-all-done.2.q_ref.oown), channel_id=1, source_target_pairs={{0,8},{8,0},{1,9},{9,1},{2,10},{10,2},{3,11},{11,3},{4,12},{12,4},... | collective-permute-start | bytes 3145736 | tf_op jit(solution)/shard_map/ppermute | solution.py:231
  137.5 14.6 %all-to-all-start.3 = ((f32[4,168,256]{2,1,0:T(8,128)}), f32[4,168,256]{2,1,0:T(8,128)S(1)}, u32[]{:S(2)}, u32[]{:S(2)}) async-start(f32[4,168,256]{2,1,0:T(8,128)} %attend.1), calls=%async_computation.3 | async-start | bytes 1376256 | tf_op jit(solution)/shard_map/all_to_all | solution.py:297

commit v3 on v2

--- a/solution.py
+++ b/solution.py
@@ -79,20 +79,22 @@
         flip_ref[j * 48 : (j + 1) * 48, :] = ot_ref[:, j * 128 : (j + 1) * 128]
 
 
-def projected(xa, xb, wown, woth):
-    zh, c = lax.axis_index("zh"), lax.axis_index("c")
+def projected(xs, wown, woth):
+    zh, x0, c = (lax.axis_index(n) for n in ("zh", "x", "c"))
     total = jnp.zeros((256, 384), F32)
     for yy in range(4):
         for w in range(2):
             slot = jnp.where(zh == 0, w, 1 - w)
             rows = []
             for z in range(2):
-                rows.append(jnp.concatenate([(xa, xb)[w][yy, z, f * 128 : (f + 1) * 128, :] for f in range(3)], axis=1))
+                tiles = [xs[yy, w * 2 + z, f * 128 : (f + 1) * 128, :] for f in range(3)]
+                rows.append(jnp.concatenate(tiles, axis=1))
             x = jnp.concatenate(rows, axis=0)
             pieces = []
             for xx in range(4):
-                own = jnp.concatenate([wown[xx, yy, slot, t * 48 : (t + 1) * 48, :] for t in range(3)], axis=1)
-                oth = jnp.concatenate([woth[xx, yy, slot, t * 48 : (t + 1) * 48, :] for t in range(3)], axis=1)
+                k = (x0 - xx) & 3
+                own = jnp.concatenate([wown[k, yy, slot, t * 48 : (t + 1) * 48, :] for t in range(3)], axis=1)
+                oth = jnp.concatenate([woth[k, yy, slot, t * 48 : (t + 1) * 48, :] for t in range(3)], axis=1)
                 pieces.append(jnp.where(c == 0, own, oth))
                 pieces.append(jnp.where(c == 0, oth, own))
             total = total + jnp.dot(x, jnp.concatenate(pieces, axis=0), preferred_element_type=F32)
@@ -104,9 +106,9 @@
     return (v * lax.rsqrt(ms + 1e-06) * gain).astype(BF)
 
 
-def project_kernel(xa, xb, wown, woth, bias, qg, kg, mine, theirs, out_ref, kv_ref):
+def project_kernel(xs, wown, woth, bias, qg, kg, mine, theirs, out_ref, kv_ref):
     zh = lax.axis_index("zh")
-    total = projected(xa, xb, wown, woth) + jnp.where(zh == 0, bias[:, :384], bias[:, 384:])
+    total = projected(xs, wown, woth) + jnp.where(zh == 0, bias[:, :384], bias[:, 384:])
     q = scaled(total[:, :128], qg[...])
     for i in range(4):
         out_ref[i, :256, :] = q
@@ -126,6 +128,12 @@
             rows = slice(part * 256 + z * 128, part * 256 + (z + 1) * 128)
             cached = jnp.where(zh == z, a, b)
             kv_ref[rows, :] = jnp.where(cached.astype(F32) < 1e29, cached, fresh[rows, :])
+
+
+def thirds(v):
+    a = v.astype(BF).astype(F32)
+    b = (v - a).astype(BF).astype(F32)
+    return a, b, v - a - b
 
 
 def attend_kernel(q_ref, kv0, kv1, bm_ref, out_ref, s_ref, mask_ref):
@@ -162,27 +170,33 @@
             mass.append(row)
             total = total + row
         out = out + tn(kv[ch % 4, 256:, :], p.astype(BF))
+    sums = jnp.concatenate(mass, axis=0)
+    high = sums.astype(BF)
+    low = (sums - high.astype(F32)).astype(BF)
+    rest = jnp.concatenate([*thirds(top), *thirds(total), jnp.zeros((10, 1024), F32)], axis=0).astype(BF)
+    out = out.astype(BF)
     for i in range(4):
         cols = slice(i * 256, (i + 1) * 256)
         out_ref[i, :128, :] = out[:, cols]
-        for r in range(32):
-            out_ref[i, 128 + r : 129 + r, :] = mass[r][:, cols]
-        out_ref[i, 160:161, :] = top[:, cols]
-        out_ref[i, 161:162, :] = total[:, cols]
-        out_ref[i, 162:168, :] = jnp.zeros((6, 256), F32)
+        out_ref[i, 128:160, :] = high[:, cols]
+        out_ref[i, 160:192, :] = low[:, cols]
+        out_ref[i, 192:208, :] = rest[:, cols]
 
 
 def merge_kernel(parts, out_ref):
     c = lax.axis_index("c")
     hi = lax.Precision.HIGHEST
-    tops = [parts[i, 160:161, :] for i in range(4)]
+    ends = [parts[i, 192:208, :].astype(F32) for i in range(4)]
+    tops = [e[0:1] + e[1:2] + e[2:3] for e in ends]
     top = jnp.maximum(jnp.maximum(tops[0], tops[1]), jnp.maximum(tops[2], tops[3]))
     factors = [jnp.exp2(t - top) for t in tops]
-    total = sum(f * parts[i, 161:162, :] for i, f in enumerate(factors))
+    total = sum(f * (e[3:4] + e[4:5] + e[5:6]) for f, e in zip(factors, ends))
     shares = [f / total for f in factors]
-    out = sum(s * parts[i, :128, :] for i, s in enumerate(shares))
+    out = sum(s * parts[i, :128, :].astype(F32) for i, s in enumerate(shares))
     att = out.T.astype(BF)
-    mass = jnp.concatenate([s * parts[i, 128:160, :] for i, s in enumerate(shares)], axis=0)
+    mass = jnp.concatenate(
+        [s * (parts[i, 128:160, :].astype(F32) + parts[i, 160:192, :].astype(F32)) for i, s in enumerate(shares)], axis=0
+    )
     i = lax.broadcasted_iota(jnp.int32, (128, 128), 0)
     b = lax.broadcasted_iota(jnp.int32, (128, 128), 1)
     cc = jnp.bitwise_xor((i >> 4) & 1, c)
@@ -193,9 +207,7 @@
     row = lax.broadcasted_iota(jnp.int32, (16, 128), 0)
     pick = ((r < 12) & ((t >> 6) == (r & 3))).astype(F32)
     m = jnp.dot(nt(pick, mass, hi), order, preferred_element_type=F32, precision=hi)
-    a = m.astype(BF).astype(F32)
-    d = (m - a).astype(BF).astype(F32)
-    e = m - a - d
+    a, d, e = thirds(m)
     packed = jnp.where(row < 4, a, jnp.where(row < 8, d, jnp.where(row < 12, e, 0.0))).astype(BF)
     out_ref[:256, :] = att
     out_ref[256:272, :] = packed
@@ -270,33 +282,32 @@
     along = spread(pay, "zl").reshape(4, 384, 128)
     toks = lax.all_gather(first, ("w", "zh"), axis=0, tiled=False)
     along, toks = lax.optimization_barrier((along, toks))
-    wown = spread(along[:, :288], "x")
-    xa = lax.all_gather(toks[:2], "y", axis=0, tiled=False)
-    wown, xa, last = lax.optimization_barrier((wown, xa, toks[2:]))
-    woth = swap(wown, "c")
+    xs = spread(toks, "y").reshape(4, 4, 384, 128)
+    wts = along[:, :288]
+    turned = [turn(wts, "x", k) for k in (1, 2, 3)]
     mine = jnp.concatenate([along[:, 288:].reshape(384, 128), sent], axis=0)
     theirs = swap(mine, "zh")
-    xb = lax.all_gather(last, "y", axis=0, tiled=False)
-    woth, theirs, xb = lax.optimization_barrier((woth, theirs, xb))
-    woth = woth.reshape(4, 4, 2, 144, 128)
+    *turned, theirs, xs = lax.optimization_barrier((*turned, theirs, xs))
+    wown = jnp.stack([wts, *turned])
+    woth = swap(wown.reshape(16, 288, 128), "c").reshape(4, 4, 2, 144, 128)
     wown = wown.reshape(4, 4, 2, 144, 128)
 
-    q, fresh = call(project_kernel, [sd((4, 1024, 128), BF), sd((512, 128), BF)], 9, limit=24, name="project")(
-        xa, xb, wown, woth, qkv_bias[None], q_gain[None], k_gain[None], mine, theirs
+    q, fresh = call(project_kernel, [sd((4, 1024, 128), BF), sd((512, 128), BF)], 8, limit=24, name="project")(
+        xs, wown, woth, qkv_bias[None], q_gain[None], k_gain[None], mine, theirs
     )
     qs = lax.all_to_all(q, "x", 0, 0, tiled=True)
     kv = call(select_kernel, sd((512, 128), BF), 3, limit=24, name="select", cover=30)(fresh, kept, theirs)
     kv0 = lax.all_gather(kv, "zl", axis=0, tiled=False)
+    kv0, qs = lax.optimization_barrier((kv0, qs))
     kv1 = swap(kv0, "c")
+    ooth = swap(qs, "c")
+    kv1, ooth = lax.optimization_barrier((kv1, ooth))
 
     parts = call(
-        attend_kernel, sd((4, 168, 256), F32), 4, [pltpu.VMEM((2048, 1024), F32), pltpu.VMEM((32, 1024), F32)],
+        attend_kernel, sd((4, 208, 256), BF), 4, [pltpu.VMEM((2048, 1024), F32), pltpu.VMEM((32, 1024), F32)],
         limit=32, name="attend",
     )(qs, kv0, kv1, block_mask)
-    late, parts = lax.optimization_barrier((qs, parts))
     parts = lax.all_to_all(parts, "x", 0, 0, tiled=True)
-    ooth = swap(late, "c")
-    parts, ooth = lax.optimization_barrier((parts, ooth))
     done = call(merge_kernel, sd((272, 128), BF), 1, limit=16, name="merge")(parts)
     rows = lax.all_gather(done, ("w", "zh"), axis=0, tiled=False)
     att = lax.all_gather(

time: 189 us -> 178 us (0.942)
  blocking collectives: 110 us -> 81.3 us
  starting transfers between devices: 49.8 us -> 59.3 us
  waiting for transfers between devices: 12.3 us -> 19.5 us
    all_gather x2 -> x0, blocking collectives: 28 us -> none  [the longest x1 14.5 us: per_device(): xb = lax.all_gather(last, 'y', axis=0, tiled=False)]
    ppermute x5, waiting for transfers between devices: 2.62 us -> 12.6 us  [swap(): return lax.ppermute(v, axis, [(0, 1), (1, 0)])]
    ppermute x0 -> x3, starting transfers between devices: none -> 8.63 us  [turn(): return lax.ppermute(v, axis, [(i, (i + k) % 4) for i in range(4)])]
    all_to_all x1, waiting for transfers between devices: 9.67 us -> 6.86 us  [per_device(): parts = lax.all_to_all(parts, 'x', 0, 0, tiled=True)]
  transfers between devices with their start and end apart: 10 -> 13, of which waited for: 3 -> 5; matrix products, arithmetic and copies ran while one was open for 0% -> 0% of each run, Pallas kernels for 0% -> 0%
where the time goes in v3:
time: 178 us; the launch traced here: 175 us
  blocking collectives  81.3 us (46%)
  starting transfers between devices  59.3 us (33%)
  waiting for transfers between devices  19.5 us (11%)
  Pallas kernels  10.6 us (6%)
  local copies, waits for them, and re-layouts  2.44 us (1%)
    all_gather x1, blocking collectives, per_device(): toks = lax.all_gather(first, ('w', 'zh'), axis=0, tiled=False)  28.5 us
    ppermute x5, starting transfers between devices, swap(): return lax.ppermute(v, axis, [(0, 1), (1, 0)])  20.6 us
    all_gather x1, blocking collectives, per_device(): rows = lax.all_gather(done, ('w', 'zh'), axis=0, tiled=False)  20.6 us
    all_gather x1, blocking collectives, per_device(): kv0 = lax.all_gather(kv, 'zl', axis=0, tiled=False)  18.8 us
    all_to_all x2, starting transfers between devices, spread(): return lax.all_to_all(wide, axis, 0, 0, tiled=True)  17.3 us
    all_gather x1, blocking collectives, per_device(): lax.all_gather(lax.dynamic_slice_in_dim(rows, lax.axis_index('zh') * 128,...  13.4 us
    ppermute x5, waiting for transfers between devices, swap(): return lax.ppermute(v, axis, [(0, 1), (1, 0)])  12.6 us
    ppermute x3, starting transfers between devices, turn(): return lax.ppermute(v, axis, [(i, (i + k) % 4) for i in range(4)])  8.63 us
  transfers between devices with their start and end apart: 13, of which 5 were waited for; matrix products, arithmetic and copies ran while one was open for 0% of the time, Pallas kernels for 0%

profile of v3, /device:TPU:6, one launch (start us, length us, event | category | flops | bytes accessed | tf_op | source)
XLA Modules:
  0.0 175.1 jit_solution(4017534545770385845)
XLA Ops:
  0.6 1.9 %prep.1 = (bf16[144,128]{1,0:T(8,128)(2,1)}, bf16[144,128]{1,0:T(8,128)(2,1)}, bf16[256,128]{1,0:T(8,128)(2,1)}, bf16[256,128]{1,0:T(8,128)(2,1)}, bf16[384,128]{1,0:T(8,128)(2,1)}, /*index=5*/bf16[96,128]{1,0:T(8,128)(2,1)}) custom-call(f32[2,2]{1,0:T(2,128)} %scale_h.1, s32[1,2]{1,0:T(1,128)} %bitcast.39, bf16[48,768]{1,0:T(8,128)(2,1)} %w_h.1, ...), custom_call_target="tpu_custom_call" | custom-call | tf_op jit(solution)/shard_map/prep/pallas_call | solution.py:261
  2.5 0.0 copy-start.4
  2.6 9.2 %collective-permute-start = (bf16[144,128]{1,0:T(8,128)(2,1)}, bf16[144,128]{1,0:T(8,128)(2,1)S(1)}, u32[]{:S(2)}, u32[]{:S(2)}) collective-permute-start(bf16[144,128]{1,0:T(8,128)(2,1)} %get-tuple-element.24), channel_id=1, source_target_pairs={{0,256},{256,0},{1,257},{257,1},{2,258},{258,2},{3,259},{259,3},{4... | collective-permute-start | bytes 110600 | tf_op jit(solution)/shard_map/ppermute | solution.py:243
  11.8 1.4 collective-permute-start.1
  13.2 0.0 collective-permute-done.1
  13.2 0.7 collective-permute-done
  13.9 0.8 pad_maximum_fusion.3
  14.7 0.8 broadcast_in_dim.27
  15.5 13.6 %all-to-all-start = ((bf16[4,384,128]{2,1,0:T(8,128)(2,1)}), bf16[4,384,128]{2,1,0:T(8,128)(2,1)S(1)}, u32[]{:S(2)}, u32[]{:S(2)}) async-start(bf16[4,384,128]{2,1,0:T(8,128)(2,1)} %broadcast_in_dim.27), calls=%async_computation | async-start | bytes 786432 | tf_op jit(solution)/shard_map/all_to_all | solution.py:248
  29.1 0.0 copy-done.4
  29.1 28.5 %all-gather = bf16[1536,128]{1,0:T(8,128)(2,1)S(1)} all-gather(bf16[384,128]{1,0:T(8,128)(2,1)S(1)} %copy-done.4), channel_id=2, replica_groups=mesh['zh'=2,'zl'=4,'x'=4,'c'=2,'w'=2,'y'=4] {'w','zh'}, dimensions={0}, use_global_device_ids=true | all-gather | bytes 491520 | tf_op jit(solution)/shard_map/all_gather | solution.py:283
  57.6 0.0 all-to-all-done
  57.6 1.5 broadcast_in_dim.28
  59.1 0.0 copy-start.5
  59.1 3.7 %all-to-all-start.1 = ((bf16[4,4,384,128]{3,2,1,0:T(8,128)(2,1)}), bf16[4,4,384,128]{3,2,1,0:T(8,128)(2,1)S(1)}, u32[]{:S(2)}, u32[]{:S(2)}) async-start(bf16[4,4,384,128]{3,2,1,0:T(8,128)(2,1)} %broadcast_in_dim.28), calls=%async_computation.1 | async-start | bytes 3145728 | tf_op jit(solution)/shard_map/all_to_all | solution.py:248
  62.8 0.1 slice_bitcast_fusion
  62.9 2.4 %collective-permute-start.2 = (bf16[4,288,128]{2,1,0:T(8,128)(2,1)S(1)}, bf16[4,288,128]{2,1,0:T(8,128)(2,1)S(1)}, u32[]{:S(2)}, u32[]{:S(2)}) collective-permute-start(bf16[4,288,128]{2,1,0:T(8,128)(2,1)S(1)} %get-tuple-element.45), channel_id=1, source_target_pairs={{0,16},{16,32},{32,48},{48,0},{1,17},{17,33},{33,49},{49,1},{2,18}... | collective-permute-start | bytes 884744 | tf_op jit(solution)/shard_map/ppermute | solution.py:252
  65.3 4.3 %collective-permute-start.3 = (bf16[4,288,128]{2,1,0:T(8,128)(2,1)S(1)}, bf16[4,288,128]{2,1,0:T(8,128)(2,1)S(1)}, u32[]{:S(2)}, u32[]{:S(2)}) collective-permute-start(bf16[4,288,128]{2,1,0:T(8,128)(2,1)S(1)} %get-tuple-element.45), channel_id=1, source_target_pairs={{0,32},{16,48},{32,0},{48,16},{1,33},{17,49},{33,1},{49,17},{2,34}... | collective-permute-start | bytes 884744 | tf_op jit(solution)/shard_map/ppermute | solution.py:252
  69.6 1.9 %collective-permute-start.4 = (bf16[4,288,128]{2,1,0:T(8,128)(2,1)S(1)}, bf16[4,288,128]{2,1,0:T(8,128)(2,1)S(1)}, u32[]{:S(2)}, u32[]{:S(2)}) collective-permute-start(bf16[4,288,128]{2,1,0:T(8,128)(2,1)S(1)} %get-tuple-element.45), channel_id=1, source_target_pairs={{0,48},{16,0},{32,16},{48,32},{1,49},{17,1},{33,17},{49,33},{2,50}... | collective-permute-start | bytes 884744 | tf_op jit(solution)/shard_map/ppermute | solution.py:252
  71.6 0.0 copy-done.5
  71.6 5.0 %collective-permute-start.5 = (bf16[640,128]{1,0:T(8,128)(2,1)S(1)}, bf16[640,128]{1,0:T(8,128)(2,1)S(1)}, u32[]{:S(2)}, u32[]{:S(2)}) collective-permute-start(bf16[640,128]{1,0:T(8,128)(2,1)S(1)} %pad_maximum_fusion.2.mine), channel_id=1, source_target_pairs={{0,256},{256,0},{1,257},{257,1},{2,258},{258,2},{3,259},{259,3},{4... | collective-permute-start | bytes 491528 | tf_op jit(solution)/shard_map/ppermute | solution.py:243
  76.7 7.8 %collective-permute-done.5.theirs = bf16[640,128]{1,0:T(8,128)(2,1)S(1)} collective-permute-done((bf16[640,128]{1,0:T(8,128)(2,1)S(1)}, bf16[640,128]{1,0:T(8,128)(2,1)S(1)}, u32[]{:S(2)}, u32[]{:S(2)}) %collective-permute-start.5) | collective-permute-done | bytes 163872 | tf_op jit(solution)/shard_map/ppermute | solution.py:243
  84.4 0.0 collective-permute-done.2
  84.4 0.0 collective-permute-done.3
  84.5 0.0 collective-permute-done.4
  84.5 0.0 all-to-all-done.1.xs
  84.5 0.0 copy-start.6
  84.5 0.2 pad_maximum_fusion.1
  84.6 1.9 %collective-permute-start.6 = (bf16[16,288,128]{2,1,0:T(8,128)(2,1)S(1)}, bf16[16,288,128]{2,1,0:T(8,128)(2,1)S(1)}, u32[]{:S(2)}, u32[]{:S(2)}) collective-permute-start(bf16[16,288,128]{2,1,0:T(8,128)(2,1)S(1)} %bitcast.36), channel_id=1, source_target_pairs={{0,8},{8,0},{1,9},{9,1},{2,10},{10,2},{3,11},{11,3},{4,12},{12,4},... | collective-permute-start | bytes 3538952 | tf_op jit(solution)/shard_map/ppermute | solution.py:243
  86.6 0.0 copy-done.6
  86.6 0.0 copy-start.1
  86.6 0.0 copy-start.2
  86.6 0.2 pad_maximum_fusion.wown
  86.8 2.6 %collective-permute-done.6 = bf16[16,288,128]{2,1,0:T(8,128)(2,1)S(1)} collective-permute-done((bf16[16,288,128]{2,1,0:T(8,128)(2,1)S(1)}, bf16[16,288,128]{2,1,0:T(8,128)(2,1)S(1)}, u32[]{:S(2)}, u32[]{:S(2)}) %collective-permute-start.6) | collective-permute-done | bytes 1179680 | tf_op jit(solution)/shard_map/ppermute | solution.py:243
  89.4 0.0 copy-done.1
  89.4 0.0 copy-done.2
  89.4 2.3 %project.1 = (bf16[4,1024,128]{2,1,0:T(8,128)(2,1)}, bf16[512,128]{1,0:T(8,128)(2,1)S(1)}) custom-call(bf16[4,4,384,128]{3,2,1,0:T(8,128)(2,1)S(1)} %all-to-all-done.1.xs, bf16[4,4,2,144,128]{4,3,2,1,0:T(8,128)(2,1)S(1)} %pad_maximum_fusion.wown, bf16[4,4,2,144,128]{4,3,2,1,0:T(8,128)(2,1)S(1)} %bitcast.25, f32[1,768]{1,0:T(1,128)S(1)} %broadcast_in_dim.29.bias, ...), custom_call_target="tpu_custom_call" | custom-call | tf_op jit(solution)/shard_map/project/pallas_call | solution.py:295
  91.7 0.0 copy-start.3
  91.7 6.6 %all-to-all-start.2 = ((bf16[4,1024,128]{2,1,0:T(8,128)(2,1)}), bf16[4,1024,128]{2,1,0:T(8,128)(2,1)S(1)}, u32[]{:S(2)}, u32[]{:S(2)}) async-start(bf16[4,1024,128]{2,1,0:T(8,128)(2,1)} %get-tuple-element.39), calls=%async_computation.2 | async-start | bytes 2097152 | tf_op jit(solution)/shard_map/all_to_all | solution.py:298
  98.2 0.0 copy-done.3
  98.2 0.0 copy-start
  98.2 0.1 select.1
  98.3 18.8 %all-gather.1 = bf16[2048,128]{1,0:T(8,128)(2,1)S(1)} all-gather(bf16[512,128]{1,0:T(8,128)(2,1)S(1)} %select.1), channel_id=3, replica_groups=mesh['zh'=2,'zl'=4,'x'=4,'c'=2,'w'=2,'y'=4] {'zl'}, dimensions={0}, use_global_device_ids=true | all-gather | bytes 655360 | tf_op jit(solution)/shard_map/all_gather | solution.py:300
  117.1 0.0 all-to-all-done.2.q_ref.oown
  117.1 0.0 copy-start.7
  117.1 0.0 copy-start.8
  117.1 2.0 %collective-permute-start.8 = (bf16[4,1024,128]{2,1,0:T(8,128)(2,1)S(1)}, bf16[4,1024,128]{2,1,0:T(8,128)(2,1)S(1)}, u32[]{:S(2)}, u32[]{:S(2)}) collective-permute-start(bf16[4,1024,128]{2,1,0:T(8,128)(2,1)S(1)} %all-to-all-done.2.q_ref.oown), channel_id=1, source_target_pairs={{0,8},{8,0},{1,9},{9,1},{2,10},{10,2},{3,11},{11,3},{4,12},{12,4},... | collective-permute-start | bytes 3145736 | tf_op jit(solution)/shard_map/ppermute | solution.py:243
  119.2 2.4 %collective-permute-start.7 = (bf16[4,512,128]{2,1,0:T(8,128)(2,1)S(1)}, bf16[4,512,128]{2,1,0:T(8,128)(2,1)S(1)}, u32[]{:S(2)}, u32[]{:S(2)}) collective-permute-start(bf16[4,512,128]{2,1,0:T(8,128)(2,1)S(1)} %bitcast.20), channel_id=1, source_target_pairs={{0,8},{8,0},{1,9},{9,1},{2,10},{10,2},{3,11},{11,3},{4,12},{12,4},... | collective-permute-start | bytes 1572872 | tf_op jit(solution)/shard_map/ppermute | solution.py:243
  121.6 1.5 collective-permute-done.7.kv1
  123.1 0.0 collective-permute-done.8.ooth
  123.1 0.0 copy-done
  123.1 4.6 %attend.1 = bf16[4,208,256]{2,1,0:T(8,128)(2,1)} custom-call(bf16[4,1024,128]{2,1,0:T(8,128)(2,1)S(1)} %all-to-all-done.2.q_ref.oown, bf16[4,512,128]{2,1,0:T(8,128)(2,1)S(1)} %bitcast.21, bf16[4,512,128]{2,1,0:T(8,128)(2,1)S(1)} %collective-permute-done.7.kv1, s32[128,128]{1,0:T(8,128)S(1)} %copy-done), custom_call_target="tpu_custom_call" | custom-call | tf_op jit(solution)/shard_map/attend/pallas_call | solution.py:306
  127.7 4.8 %all-to-all-start.3 = ((bf16[4,208,256]{2,1,0:T(8,128)(2,1)}), bf16[4,208,256]{2,1,0:T(8,128)(2,1)S(1)}, u32[]{:S(2)}, u32[]{:S(2)}) async-start(bf16[4,208,256]{2,1,0:T(8,128)(2,1)} %attend.1), calls=%async_computation.3 | async-start | bytes 851968 | tf_op jit(solution)/shard_map/all_to_all | solution.py:310
  132.5 0.0 copy-done.7
  132.5 0.0 copy-done.8
  132.5 6.9 %all-to-all-done.3.parts = bf16[4,208,256]{2,1,0:T(8,128)(2,1)S(1)} async-done(((bf16[4,208,256]{2,1,0:T(8,128)(2,1)}), bf16[4,208,256]{2,1,0:T(8,128)(2,1)S(1)}, u32[]{:S(2)}, u32[]{:S(2)}) %all-to-all-start.3) | async-done | bytes 426016 | tf_op jit(solution)/shard_map/all_to_all | solution.py:310
  139.4 0.5 merge.1
  139.9 20.6 %all-gather.2 = bf16[1088,128]{1,0:T(8,128)(2,1)S(1)} all-gather(bf16[272,128]{1,0:T(8,128)(2,1)S(1)} %merge.1), channel_id=4, replica_groups=mesh['zh'=2,'zl'=4,'x'=4,'c'=2,'w'=2,'y'=4] {'w','zh'}, dimensions={0}, use_global_device_ids=true | all-gather | bytes 348160 | tf_op jit(solution)/shard_map/all_gather | solution.py:312
  160.5 13.4 %all-gather.3 = bf16[16,128,128]{2,1,0:T(8,128)(2,1)S(1)} all-gather(bf16[4,128,128]{2,1,0:T(8,128)(2,1)S(1)} %constant_dynamic-slice_fusion), channel_id=5, replica_groups=mesh['zh'=2,'zl'=4,'x'=4,'c'=2,'w'=2,'y'=4] {'y'}, dimensions={0}, use_global_device_ids=true | all-gather | bytes 655360 | tf_op jit(solution)/shard_map/all_gather | solution.py:313
  173.9 1.3 finish.1
  (6 shorter events, 0.0 us)
Async XLA Ops:
  2.5 26.6 %copy-start.4 = (bf16[384,128]{1,0:T(8,128)(2,1)S(1)}, bf16[384,128]{1,0:T(8,128)(2,1)}, u32[]{:S(2)}) copy-start(bf16[384,128]{1,0:T(8,128)(2,1)} %get-tuple-element.28) | copy-start | bytes 294916
  2.6 11.4 %collective-permute-start = (bf16[144,128]{1,0:T(8,128)(2,1)}, bf16[144,128]{1,0:T(8,128)(2,1)S(1)}, u32[]{:S(2)}, u32[]{:S(2)}) collective-permute-start(bf16[144,128]{1,0:T(8,128)(2,1)} %get-tuple-element.24), channel_id=1, source_target_pairs={{0,256},{256,0},{1,257},{257,1},{2,258},{258,2},{3,259},{259,3},{4... | collective-permute-start | bytes 110600 | tf_op jit(solution)/shard_map/ppermute | solution.py:243
  11.8 1.4 collective-permute-start.1
  15.5 42.1 %all-to-all-start = ((bf16[4,384,128]{2,1,0:T(8,128)(2,1)}), bf16[4,384,128]{2,1,0:T(8,128)(2,1)S(1)}, u32[]{:S(2)}, u32[]{:S(2)}) async-start(bf16[4,384,128]{2,1,0:T(8,128)(2,1)} %broadcast_in_dim.27), calls=%async_computation | async-start | bytes 786432 | tf_op jit(solution)/shard_map/all_to_all | solution.py:248
  59.1 12.5 %copy-start.5 = (bf16[256,128]{1,0:T(8,128)(2,1)S(1)}, bf16[256,128]{1,0:T(8,128)(2,1)}, u32[]{:S(2)}) copy-start(bf16[256,128]{1,0:T(8,128)(2,1)} %get-tuple-element.30) | copy-start | bytes 196612
  59.1 25.3 %all-to-all-start.1 = ((bf16[4,4,384,128]{3,2,1,0:T(8,128)(2,1)}), bf16[4,4,384,128]{3,2,1,0:T(8,128)(2,1)S(1)}, u32[]{:S(2)}, u32[]{:S(2)}) async-start(bf16[4,4,384,128]{3,2,1,0:T(8,128)(2,1)} %broadcast_in_dim.28), calls=%async_computation.1 | async-start | bytes 3145728 | tf_op jit(solution)/shard_map/all_to_all | solution.py:248
  62.9 21.5 %collective-permute-start.2 = (bf16[4,288,128]{2,1,0:T(8,128)(2,1)S(1)}, bf16[4,288,128]{2,1,0:T(8,128)(2,1)S(1)}, u32[]{:S(2)}, u32[]{:S(2)}) collective-permute-start(bf16[4,288,128]{2,1,0:T(8,128)(2,1)S(1)} %get-tuple-element.45), channel_id=1, source_target_pairs={{0,16},{16,32},{32,48},{48,0},{1,17},{17,33},{33,49},{49,1},{2,18}... | collective-permute-start | bytes 884744 | tf_op jit(solution)/shard_map/ppermute | solution.py:252
  65.3 19.1 %collective-permute-start.3 = (bf16[4,288,128]{2,1,0:T(8,128)(2,1)S(1)}, bf16[4,288,128]{2,1,0:T(8,128)(2,1)S(1)}, u32[]{:S(2)}, u32[]{:S(2)}) collective-permute-start(bf16[4,288,128]{2,1,0:T(8,128)(2,1)S(1)} %get-tuple-element.45), channel_id=1, source_target_pairs={{0,32},{16,48},{32,0},{48,16},{1,33},{17,49},{33,1},{49,17},{2,34}... | collective-permute-start | bytes 884744 | tf_op jit(solution)/shard_map/ppermute | solution.py:252
  69.6 14.8 %collective-permute-start.4 = (bf16[4,288,128]{2,1,0:T(8,128)(2,1)S(1)}, bf16[4,288,128]{2,1,0:T(8,128)(2,1)S(1)}, u32[]{:S(2)}, u32[]{:S(2)}) collective-permute-start(bf16[4,288,128]{2,1,0:T(8,128)(2,1)S(1)} %get-tuple-element.45), channel_id=1, source_target_pairs={{0,48},{16,0},{32,16},{48,32},{1,49},{17,1},{33,17},{49,33},{2,50}... | collective-permute-start | bytes 884744 | tf_op jit(solution)/shard_map/ppermute | solution.py:252
  71.6 12.8 %collective-permute-start.5 = (bf16[640,128]{1,0:T(8,128)(2,1)S(1)}, bf16[640,128]{1,0:T(8,128)(2,1)S(1)}, u32[]{:S(2)}, u32[]{:S(2)}) collective-permute-start(bf16[640,128]{1,0:T(8,128)(2,1)S(1)} %pad_maximum_fusion.2.mine), channel_id=1, source_target_pairs={{0,256},{256,0},{1,257},{257,1},{2,258},{258,2},{3,259},{259,3},{4... | collective-permute-start | bytes 491528 | tf_op jit(solution)/shard_map/ppermute | solution.py:243
  84.5 2.1 %copy-start.6 = (f32[768]{0:T(1024)S(1)}, f32[768]{0:T(1024)}, u32[]{:S(2)}) copy-start(f32[768]{0:T(1024)} %param.14) | copy-start | bytes 9220
  84.6 4.7 %collective-permute-start.6 = (bf16[16,288,128]{2,1,0:T(8,128)(2,1)S(1)}, bf16[16,288,128]{2,1,0:T(8,128)(2,1)S(1)}, u32[]{:S(2)}, u32[]{:S(2)}) collective-permute-start(bf16[16,288,128]{2,1,0:T(8,128)(2,1)S(1)} %bitcast.36), channel_id=1, source_target_pairs={{0,8},{8,0},{1,9},{9,1},{2,10},{10,2},{3,11},{11,3},{4,12},{12,4},... | collective-permute-start | bytes 3538952 | tf_op jit(solution)/shard_map/ppermute | solution.py:243
  86.6 2.8 %copy-start.1 = (f32[128]{0:T(128)S(1)}, f32[128]{0:T(128)}, u32[]{:S(2)}) copy-start(f32[128]{0:T(128)} %param.15) | copy-start | bytes 1540
  86.6 2.8 %copy-start.2 = (f32[128]{0:T(128)S(1)}, f32[128]{0:T(128)}, u32[]{:S(2)}) copy-start(f32[128]{0:T(128)} %param.16) | copy-start | bytes 1540
  91.7 6.6 %copy-start.3 = (bf16[256,128]{1,0:T(8,128)(2,1)S(1)}, bf16[256,128]{1,0:T(8,128)(2,1)}, u32[]{:S(2)}) copy-start(bf16[256,128]{1,0:T(8,128)(2,1)} %get-tuple-element.38.kept) | copy-start | bytes 196612
  91.7 25.4 %all-to-all-start.2 = ((bf16[4,1024,128]{2,1,0:T(8,128)(2,1)}), bf16[4,1024,128]{2,1,0:T(8,128)(2,1)S(1)}, u32[]{:S(2)}, u32[]{:S(2)}) async-start(bf16[4,1024,128]{2,1,0:T(8,128)(2,1)} %get-tuple-element.39), calls=%async_computation.2 | async-start | bytes 2097152 | tf_op jit(solution)/shard_map/all_to_all | solution.py:298
  98.2 24.9 %copy-start = (s32[128,128]{1,0:T(8,128)S(1)}, s32[128,128]{1,0:T(8,128)}, u32[]{:S(2)}) copy-start(s32[128,128]{1,0:T(8,128)} %bm_ref.1) | copy-start | bytes 196612
  117.1 15.4 %copy-start.7 = (f32[384]{0:T(512)S(1)}, f32[384]{0:T(512)}, u32[]{:S(2)}) copy-start(f32[384]{0:T(512)} %param.22) | copy-start | bytes 4612
  117.1 15.4 %copy-start.8 = (f32[384]{0:T(512)S(1)}, f32[384]{0:T(512)}, u32[]{:S(2)}) copy-start(f32[384]{0:T(512)} %param.23) | copy-start | bytes 4612
  117.1 6.0 %collective-permute-start.8 = (bf16[4,1024,128]{2,1,0:T(8,128)(2,1)S(1)}, bf16[4,1024,128]{2,1,0:T(8,128)(2,1)S(1)}, u32[]{:S(2)}, u32[]{:S(2)}) collective-permute-start(bf16[4,1024,128]{2,1,0:T(8,128)(2,1)S(1)} %all-to-all-done.2.q_ref.oown), channel_id=1, source_target_pairs={{0,8},{8,0},{1,9},{9,1},{2,10},{10,2},{3,11},{11,3},{4,12},{12,4},... | collective-permute-start | bytes 3145736 | tf_op jit(solution)/shard_map/ppermute | solution.py:243
  119.2 3.9 %collective-permute-start.7 = (bf16[4,512,128]{2,1,0:T(8,128)(2,1)S(1)}, bf16[4,512,128]{2,1,0:T(8,128)(2,1)S(1)}, u32[]{:S(2)}, u32[]{:S(2)}) collective-permute-start(bf16[4,512,128]{2,1,0:T(8,128)(2,1)S(1)} %bitcast.20), channel_id=1, source_target_pairs={{0,8},{8,0},{1,9},{9,1},{2,10},{10,2},{3,11},{11,3},{4,12},{12,4},... | collective-permute-start | bytes 1572872 | tf_op jit(solution)/shard_map/ppermute | solution.py:243
  127.7 11.7 %all-to-all-start.3 = ((bf16[4,208,256]{2,1,0:T(8,128)(2,1)}), bf16[4,208,256]{2,1,0:T(8,128)(2,1)S(1)}, u32[]{:S(2)}, u32[]{:S(2)}) async-start(bf16[4,208,256]{2,1,0:T(8,128)(2,1)} %attend.1), calls=%async_computation.3 | async-start | bytes 851968 | tf_op jit(solution)/shard_map/all_to_all | solution.py:310

commit v4 on v3

--- a/solution.py
+++ b/solution.py
@@ -20,14 +20,14 @@
 HB = pl.BlockSpec(memory_space=pltpu.HBM)
 
 
-def call(kernel, outs, n_in, scratch=(), place=VM, limit=48, name=None, cover=0):
+def call(kernel, outs, n_in, scratch=(), place=VM, limit=48, name=None, cover=0, first=VM):
     multiple = isinstance(outs, (list, tuple))
     cost = pl.CostEstimate(flops=cover * 10**9, bytes_accessed=0, transcendentals=0) if cover else None
     return pl.pallas_call(
         kernel,
         out_shape=outs,
         in_specs=[place] * n_in,
-        out_specs=[VM] * len(outs) if multiple else VM,
+        out_specs=[first] + [VM] * (len(outs) - 1) if multiple else VM,
         scratch_shapes=list(scratch),
         compiler_params=pltpu.CompilerParams(vmem_limit_bytes=limit * 1024 * 1024 if limit else None),
         cost_estimate=cost,
@@ -79,6 +79,10 @@
         flip_ref[j * 48 : (j + 1) * 48, :] = ot_ref[:, j * 128 : (j + 1) * 128]
 
 
+def bias_kernel(bias, out_ref):
+    out_ref[...] = jnp.where(lax.axis_index("zh") == 0, bias[:, :384], bias[:, 384:])
+
+
 def projected(xs, wown, woth):
     zh, x0, c = (lax.axis_index(n) for n in ("zh", "x", "c"))
     total = jnp.zeros((256, 384), F32)
@@ -106,17 +110,19 @@
     return (v * lax.rsqrt(ms + 1e-06) * gain).astype(BF)
 
 
-def project_kernel(xs, wown, woth, bias, qg, kg, mine, theirs, out_ref, kv_ref):
-    zh = lax.axis_index("zh")
-    total = projected(xs, wown, woth) + jnp.where(zh == 0, bias[:, :384], bias[:, 384:])
-    q = scaled(total[:, :128], qg[...])
-    for i in range(4):
-        out_ref[i, :256, :] = q
-        for z in range(4):
-            out_ref[i, 256 + z * 192 : 352 + z * 192, :] = mine[z * 96 : (z + 1) * 96, :]
-            out_ref[i, 352 + z * 192 : 448 + z * 192, :] = theirs[z * 96 : (z + 1) * 96, :]
+def project_kernel(xs, wown, woth, bias, qg, kg, mine, theirs, out_ref, kv_ref, tile, sems):
+    total = projected(xs, wown, woth) + bias[...]
+    tile[:256, :] = scaled(total[:, :128], qg[...])
+    for z in range(4):
+        tile[256 + z * 192 : 352 + z * 192, :] = mine[z * 96 : (z + 1) * 96, :]
+        tile[352 + z * 192 : 448 + z * 192, :] = theirs[z * 96 : (z + 1) * 96, :]
+    copies = [pltpu.make_async_copy(tile, out_ref.at[i], sems.at[i]) for i in range(4)]
+    for copy in copies:
+        copy.start()
     kv_ref[:256, :] = scaled(total[:, 128:256], kg[...])
     kv_ref[256:, :] = total[:, 256:].astype(BF)
+    for copy in copies:
+        copy.wait()
 
 
 def select_kernel(fresh, kept, theirs, kv_ref):
@@ -287,13 +293,17 @@
     turned = [turn(wts, "x", k) for k in (1, 2, 3)]
     mine = jnp.concatenate([along[:, 288:].reshape(384, 128), sent], axis=0)
     theirs = swap(mine, "zh")
-    *turned, theirs, xs = lax.optimization_barrier((*turned, theirs, xs))
     wown = jnp.stack([wts, *turned])
     woth = swap(wown.reshape(16, 288, 128), "c").reshape(4, 4, 2, 144, 128)
+    xs, theirs, bias = lax.optimization_barrier((xs, theirs, qkv_bias[None]))
+    bias = call(bias_kernel, sd((1, 384), F32), 1, limit=16, name="bias", cover=40)(bias)
+    xs, theirs, bias = lax.optimization_barrier((xs, theirs, bias))
     wown = wown.reshape(4, 4, 2, 144, 128)
 
-    q, fresh = call(project_kernel, [sd((4, 1024, 128), BF), sd((512, 128), BF)], 8, limit=24, name="project")(
-        xs, wown, woth, qkv_bias[None], q_gain[None], k_gain[None], mine, theirs
+    q, fresh = call(project_kernel, [sd((4, 1024, 128), BF), sd((512, 128), BF)], 8,
+        [pltpu.VMEM((1024, 128), BF), pltpu.SemaphoreType.DMA((4,))], limit=24, name="project", first=HB,
+    )(
+        xs, wown, woth, bias, q_gain[None], k_gain[None], mine, theirs
     )
     qs = lax.all_to_all(q, "x", 0, 0, tiled=True)
     kv = call(select_kernel, sd((512, 128), BF), 3, limit=24, name="select", cover=30)(fresh, kept, theirs)

time: 178 us -> 175 us (0.983)
  waiting for transfers between devices: 19.5 us -> 13.3 us
    ppermute x5, waiting for transfers between devices: 12.6 us -> 5.61 us  [swap(): return lax.ppermute(v, axis, [(0, 1), (1, 0)])]
  transfers between devices with their start and end apart: 13 -> 13, of which waited for: 5 -> 5; matrix products, arithmetic and copies ran while one was open for 0% -> 1% of each run, Pallas kernels for 0% -> 0%
where the time goes in v4:
time: 175 us; the launch traced here: 172 us
  blocking collectives  81.6 us (47%)
  starting transfers between devices  59.8 us (34%)
  waiting for transfers between devices  13.3 us (8%)
  Pallas kernels  11 us (6%)
  local copies, waits for them, and re-layouts  3.43 us (2%)
  other arithmetic  2.12 us (1%)
    all_gather x1, blocking collectives, per_device(): toks = lax.all_gather(first, ('w', 'zh'), axis=0, tiled=False)  28.5 us
    ppermute x5, starting transfers between devices, swap(): return lax.ppermute(v, axis, [(0, 1), (1, 0)])  20.6 us
    all_gather x1, blocking collectives, per_device(): rows = lax.all_gather(done, ('w', 'zh'), axis=0, tiled=False)  19.9 us
    all_gather x1, blocking collectives, per_device(): kv0 = lax.all_gather(kv, 'zl', axis=0, tiled=False)  19.4 us
    all_to_all x2, starting transfers between devices, spread(): return lax.all_to_all(wide, axis, 0, 0, tiled=True)  17.3 us
    all_gather x1, blocking collectives, per_device(): lax.all_gather(lax.dynamic_slice_in_dim(rows, lax.axis_index('zh') * 128,...  13.8 us
    ppermute x3, starting transfers between devices, turn(): return lax.ppermute(v, axis, [(i, (i + k) % 4) for i in range(4)])  9.76 us
    all_to_all x1, waiting for transfers between devices, per_device(): parts = lax.all_to_all(parts, 'x', 0, 0, tiled=True)  6.86 us
  transfers between devices with their start and end apart: 13, of which 5 were waited for; matrix products, arithmetic and copies ran while one was open for 1% of the time, Pallas kernels for 0%

profile of v4, /device:TPU:6, one launch (start us, length us, event | category | flops | bytes accessed | tf_op | source)
XLA Modules:
  0.0 172.1 jit_solution(11516820484824611050)
XLA Ops:
  0.6 1.9 %prep.1 = (bf16[144,128]{1,0:T(8,128)(2,1)}, bf16[144,128]{1,0:T(8,128)(2,1)}, bf16[256,128]{1,0:T(8,128)(2,1)}, bf16[256,128]{1,0:T(8,128)(2,1)}, bf16[384,128]{1,0:T(8,128)(2,1)}, /*index=5*/bf16[96,128]{1,0:T(8,128)(2,1)}) custom-call(f32[2,2]{1,0:T(2,128)} %scale_h.1, s32[1,2]{1,0:T(1,128)} %bitcast.37, bf16[48,768]{1,0:T(8,128)(2,1)} %w_h.1, ...), custom_call_target="tpu_custom_call" | custom-call | tf_op jit(solution)/shard_map/prep/pallas_call | solution.py:267
  2.5 0.0 copy-start.5
  2.6 9.2 %collective-permute-start = (bf16[144,128]{1,0:T(8,128)(2,1)}, bf16[144,128]{1,0:T(8,128)(2,1)S(1)}, u32[]{:S(2)}, u32[]{:S(2)}) collective-permute-start(bf16[144,128]{1,0:T(8,128)(2,1)} %get-tuple-element.25), channel_id=1, source_target_pairs={{0,256},{256,0},{1,257},{257,1},{2,258},{258,2},{3,259},{259,3},{4... | collective-permute-start | bytes 110600 | tf_op jit(solution)/shard_map/ppermute | solution.py:249
  11.8 1.4 collective-permute-start.1
  13.2 0.0 collective-permute-done.1
  13.2 0.7 collective-permute-done
  13.9 0.8 pad_maximum_fusion.3
  14.7 0.8 broadcast_in_dim.27
  15.5 13.6 %all-to-all-start = ((bf16[4,384,128]{2,1,0:T(8,128)(2,1)}), bf16[4,384,128]{2,1,0:T(8,128)(2,1)S(1)}, u32[]{:S(2)}, u32[]{:S(2)}) async-start(bf16[4,384,128]{2,1,0:T(8,128)(2,1)} %broadcast_in_dim.27), calls=%async_computation | async-start | bytes 786432 | tf_op jit(solution)/shard_map/all_to_all | solution.py:254
  29.1 0.0 copy-done.5
  29.1 28.5 %all-gather = bf16[1536,128]{1,0:T(8,128)(2,1)S(1)} all-gather(bf16[384,128]{1,0:T(8,128)(2,1)S(1)} %copy-done.5), channel_id=2, replica_groups=mesh['zh'=2,'zl'=4,'x'=4,'c'=2,'w'=2,'y'=4] {'w','zh'}, dimensions={0}, use_global_device_ids=true | all-gather | bytes 491520 | tf_op jit(solution)/shard_map/all_gather | solution.py:289
  57.6 0.0 all-to-all-done
  57.6 1.5 broadcast_in_dim.28
  59.1 0.0 copy-start.7
  59.1 0.0 copy-start.6
  59.1 3.7 %all-to-all-start.1 = ((bf16[4,4,384,128]{3,2,1,0:T(8,128)(2,1)}), bf16[4,4,384,128]{3,2,1,0:T(8,128)(2,1)S(1)}, u32[]{:S(2)}, u32[]{:S(2)}) async-start(bf16[4,4,384,128]{3,2,1,0:T(8,128)(2,1)} %broadcast_in_dim.28), calls=%async_computation.1 | async-start | bytes 3145728 | tf_op jit(solution)/shard_map/all_to_all | solution.py:254
  62.8 0.1 slice_bitcast_fusion
  62.9 2.7 %collective-permute-start.5 = (bf16[4,288,128]{2,1,0:T(8,128)(2,1)S(1)}, bf16[4,288,128]{2,1,0:T(8,128)(2,1)S(1)}, u32[]{:S(2)}, u32[]{:S(2)}) collective-permute-start(bf16[4,288,128]{2,1,0:T(8,128)(2,1)S(1)} %get-tuple-element.47), channel_id=1, source_target_pairs={{0,48},{16,0},{32,16},{48,32},{1,49},{17,1},{33,17},{49,33},{2,50}... | collective-permute-start | bytes 884744 | tf_op jit(solution)/shard_map/ppermute | solution.py:258
  65.7 3.0 %collective-permute-start.4 = (bf16[4,288,128]{2,1,0:T(8,128)(2,1)S(1)}, bf16[4,288,128]{2,1,0:T(8,128)(2,1)S(1)}, u32[]{:S(2)}, u32[]{:S(2)}) collective-permute-start(bf16[4,288,128]{2,1,0:T(8,128)(2,1)S(1)} %get-tuple-element.47), channel_id=1, source_target_pairs={{0,32},{16,48},{32,0},{48,16},{1,33},{17,49},{33,1},{49,17},{2,34}... | collective-permute-start | bytes 884744 | tf_op jit(solution)/shard_map/ppermute | solution.py:258
  68.7 4.0 %collective-permute-start.3 = (bf16[4,288,128]{2,1,0:T(8,128)(2,1)S(1)}, bf16[4,288,128]{2,1,0:T(8,128)(2,1)S(1)}, u32[]{:S(2)}, u32[]{:S(2)}) collective-permute-start(bf16[4,288,128]{2,1,0:T(8,128)(2,1)S(1)} %get-tuple-element.47), channel_id=1, source_target_pairs={{0,16},{16,32},{32,48},{48,0},{1,17},{17,33},{33,49},{49,1},{2,18}... | collective-permute-start | bytes 884744 | tf_op jit(solution)/shard_map/ppermute | solution.py:258
  72.7 0.0 copy-done.7
  72.8 0.0 copy-done.6
  72.8 5.0 %collective-permute-start.2 = (bf16[640,128]{1,0:T(8,128)(2,1)S(1)}, bf16[640,128]{1,0:T(8,128)(2,1)S(1)}, u32[]{:S(2)}, u32[]{:S(2)}) collective-permute-start(bf16[640,128]{1,0:T(8,128)(2,1)S(1)} %pad_maximum_fusion.2.mine), channel_id=1, source_target_pairs={{0,256},{256,0},{1,257},{257,1},{2,258},{258,2},{3,259},{259,3},{4... | collective-permute-start | bytes 491528 | tf_op jit(solution)/shard_map/ppermute | solution.py:249
  77.8 0.0 collective-permute-done.5
  77.8 0.0 collective-permute-done.4
  77.8 0.8 collective-permute-done.3
  78.7 1.2 pad_maximum_fusion.1
  79.9 1.9 %collective-permute-start.6 = (bf16[16,288,128]{2,1,0:T(8,128)(2,1)}, bf16[16,288,128]{2,1,0:T(8,128)(2,1)}, u32[]{:S(2)}, u32[]{:S(2)}) collective-permute-start(bf16[16,288,128]{2,1,0:T(8,128)(2,1)} %bitcast.12), channel_id=1, source_target_pairs={{0,8},{8,0},{1,9},{9,1},{2,10},{10,2},{3,11},{11,3},{4,12},{12,4},... | collective-permute-start | bytes 3538952 | tf_op jit(solution)/shard_map/ppermute | solution.py:249
  81.8 0.2 pad_maximum_fusion.wown
  81.9 0.0 copy-start.2
  82.0 0.0 copy-start.3
  82.0 3.4 %collective-permute-done.2.theirs = bf16[640,128]{1,0:T(8,128)(2,1)S(1)} collective-permute-done((bf16[640,128]{1,0:T(8,128)(2,1)S(1)}, bf16[640,128]{1,0:T(8,128)(2,1)S(1)}, u32[]{:S(2)}, u32[]{:S(2)}) %collective-permute-start.2) | collective-permute-done | bytes 163872 | tf_op jit(solution)/shard_map/ppermute | solution.py:249
  85.3 0.0 all-to-all-done.1.xs
  85.3 0.0 collective-permute-done.6
  85.3 0.0 copy-done.2
  85.4 0.0 copy-done.3
  85.4 2.7 %project.1 = (bf16[4,1024,128]{2,1,0:T(8,128)(2,1)S(1)}, bf16[512,128]{1,0:T(8,128)(2,1)S(1)}) custom-call(bf16[4,4,384,128]{3,2,1,0:T(8,128)(2,1)S(1)} %all-to-all-done.1.xs, bf16[4,4,2,144,128]{4,3,2,1,0:T(8,128)(2,1)S(1)} %pad_maximum_fusion.wown, bf16[4,4,2,144,128]{4,3,2,1,0:T(8,128)(2,1)} %bitcast.13.woth, f32[1,384]{1,0:T(1,128)S(1)} %bias.1, ...), custom_call_target="tpu_custom_call" | custom-call | tf_op jit(solution)/shard_map/project/pallas_call | solution.py:303
  88.1 0.0 copy-start
  88.1 1.0 copy-done
  89.1 0.0 copy-start.4
  89.1 5.9 %all-to-all-start.2 = ((bf16[4,1024,128]{2,1,0:T(8,128)(2,1)}), bf16[4,1024,128]{2,1,0:T(8,128)(2,1)S(1)}, u32[]{:S(2)}, u32[]{:S(2)}) async-start(bf16[4,1024,128]{2,1,0:T(8,128)(2,1)} %copy-done), calls=%async_computation.2 | async-start | bytes 2097152 | tf_op jit(solution)/shard_map/all_to_all | solution.py:308
  95.0 0.0 copy-done.4
  95.0 0.0 copy-start.1
  95.0 0.1 select.1
  95.0 19.4 %all-gather.1 = bf16[2048,128]{1,0:T(8,128)(2,1)S(1)} all-gather(bf16[512,128]{1,0:T(8,128)(2,1)S(1)} %select.1), channel_id=3, replica_groups=mesh['zh'=2,'zl'=4,'x'=4,'c'=2,'w'=2,'y'=4] {'zl'}, dimensions={0}, use_global_device_ids=true | all-gather | bytes 655360 | tf_op jit(solution)/shard_map/all_gather | solution.py:310
  114.4 0.0 all-to-all-done.2.q_ref.oown
  114.5 0.0 copy-start.8
  114.5 0.0 copy-start.9
  114.5 2.0 %collective-permute-start.8 = (bf16[4,1024,128]{2,1,0:T(8,128)(2,1)S(1)}, bf16[4,1024,128]{2,1,0:T(8,128)(2,1)S(1)}, u32[]{:S(2)}, u32[]{:S(2)}) collective-permute-start(bf16[4,1024,128]{2,1,0:T(8,128)(2,1)S(1)} %all-to-all-done.2.q_ref.oown), channel_id=1, source_target_pairs={{0,8},{8,0},{1,9},{9,1},{2,10},{10,2},{3,11},{11,3},{4,12},{12,4},... | collective-permute-start | bytes 3145736 | tf_op jit(solution)/shard_map/ppermute | solution.py:249
  116.5 2.4 %collective-permute-start.7 = (bf16[4,512,128]{2,1,0:T(8,128)(2,1)S(1)}, bf16[4,512,128]{2,1,0:T(8,128)(2,1)S(1)}, u32[]{:S(2)}, u32[]{:S(2)}) collective-permute-start(bf16[4,512,128]{2,1,0:T(8,128)(2,1)S(1)} %bitcast.20), channel_id=1, source_target_pairs={{0,8},{8,0},{1,9},{9,1},{2,10},{10,2},{3,11},{11,3},{4,12},{12,4},... | collective-permute-start | bytes 1572872 | tf_op jit(solution)/shard_map/ppermute | solution.py:249
  118.9 1.5 collective-permute-done.7.kv1
  120.4 0.0 collective-permute-done.8.ooth
  120.4 0.0 copy-done.1
  120.4 4.6 %attend.1 = bf16[4,208,256]{2,1,0:T(8,128)(2,1)} custom-call(bf16[4,1024,128]{2,1,0:T(8,128)(2,1)S(1)} %all-to-all-done.2.q_ref.oown, bf16[4,512,128]{2,1,0:T(8,128)(2,1)S(1)} %bitcast.21, bf16[4,512,128]{2,1,0:T(8,128)(2,1)S(1)} %collective-permute-done.7.kv1, s32[128,128]{1,0:T(8,128)S(1)} %copy-done.1), custom_call_target="tpu_custom_call" | custom-call | tf_op jit(solution)/shard_map/attend/pallas_call | solution.py:316
  125.1 4.8 %all-to-all-start.3 = ((bf16[4,208,256]{2,1,0:T(8,128)(2,1)}), bf16[4,208,256]{2,1,0:T(8,128)(2,1)S(1)}, u32[]{:S(2)}, u32[]{:S(2)}) async-start(bf16[4,208,256]{2,1,0:T(8,128)(2,1)} %attend.1), calls=%async_computation.3 | async-start | bytes 851968 | tf_op jit(solution)/shard_map/all_to_all | solution.py:320
  129.9 0.0 copy-done.8
  129.9 0.0 copy-done.9
  129.9 6.9 %all-to-all-done.3.parts = bf16[4,208,256]{2,1,0:T(8,128)(2,1)S(1)} async-done(((bf16[4,208,256]{2,1,0:T(8,128)(2,1)}), bf16[4,208,256]{2,1,0:T(8,128)(2,1)S(1)}, u32[]{:S(2)}, u32[]{:S(2)}) %all-to-all-start.3) | async-done | bytes 426016 | tf_op jit(solution)/shard_map/all_to_all | solution.py:320
  136.7 0.5 merge.1
  137.2 19.9 %all-gather.2 = bf16[1088,128]{1,0:T(8,128)(2,1)S(1)} all-gather(bf16[272,128]{1,0:T(8,128)(2,1)S(1)} %merge.1), channel_id=4, replica_groups=mesh['zh'=2,'zl'=4,'x'=4,'c'=2,'w'=2,'y'=4] {'w','zh'}, dimensions={0}, use_global_device_ids=true | all-gather | bytes 348160 | tf_op jit(solution)/shard_map/all_gather | solution.py:322
  157.1 13.8 %all-gather.3 = bf16[16,128,128]{2,1,0:T(8,128)(2,1)S(1)} all-gather(bf16[4,128,128]{2,1,0:T(8,128)(2,1)S(1)} %constant_dynamic-slice_fusion), channel_id=5, replica_groups=mesh['zh'=2,'zl'=4,'x'=4,'c'=2,'w'=2,'y'=4] {'y'}, dimensions={0}, use_global_device_ids=true | all-gather | bytes 655360 | tf_op jit(solution)/shard_map/all_gather | solution.py:323
  170.9 1.3 finish.1
  (7 shorter events, 0.0 us)
Async XLA Ops:
  2.5 26.6 %copy-start.5 = (bf16[384,128]{1,0:T(8,128)(2,1)S(1)}, bf16[384,128]{1,0:T(8,128)(2,1)}, u32[]{:S(2)}) copy-start(bf16[384,128]{1,0:T(8,128)(2,1)} %get-tuple-element.29) | copy-start | bytes 294916
  2.6 11.4 %collective-permute-start = (bf16[144,128]{1,0:T(8,128)(2,1)}, bf16[144,128]{1,0:T(8,128)(2,1)S(1)}, u32[]{:S(2)}, u32[]{:S(2)}) collective-permute-start(bf16[144,128]{1,0:T(8,128)(2,1)} %get-tuple-element.25), channel_id=1, source_target_pairs={{0,256},{256,0},{1,257},{257,1},{2,258},{258,2},{3,259},{259,3},{4... | collective-permute-start | bytes 110600 | tf_op jit(solution)/shard_map/ppermute | solution.py:249
  11.8 1.4 collective-permute-start.1
  15.5 42.1 %all-to-all-start = ((bf16[4,384,128]{2,1,0:T(8,128)(2,1)}), bf16[4,384,128]{2,1,0:T(8,128)(2,1)S(1)}, u32[]{:S(2)}, u32[]{:S(2)}) async-start(bf16[4,384,128]{2,1,0:T(8,128)(2,1)} %broadcast_in_dim.27), calls=%async_computation | async-start | bytes 786432 | tf_op jit(solution)/shard_map/all_to_all | solution.py:254
  59.1 13.6 %copy-start.7 = (f32[768]{0:T(1024)S(1)}, f32[768]{0:T(1024)}, u32[]{:S(2)}) copy-start(f32[768]{0:T(1024)} %param.14) | copy-start | bytes 9220
  59.1 13.6 %copy-start.6 = (bf16[256,128]{1,0:T(8,128)(2,1)S(1)}, bf16[256,128]{1,0:T(8,128)(2,1)}, u32[]{:S(2)}) copy-start(bf16[256,128]{1,0:T(8,128)(2,1)} %get-tuple-element.32) | copy-start | bytes 196612
  59.1 26.2 %all-to-all-start.1 = ((bf16[4,4,384,128]{3,2,1,0:T(8,128)(2,1)}), bf16[4,4,384,128]{3,2,1,0:T(8,128)(2,1)S(1)}, u32[]{:S(2)}, u32[]{:S(2)}) async-start(bf16[4,4,384,128]{3,2,1,0:T(8,128)(2,1)} %broadcast_in_dim.28), calls=%async_computation.1 | async-start | bytes 3145728 | tf_op jit(solution)/shard_map/all_to_all | solution.py:254
  62.9 14.9 %collective-permute-start.5 = (bf16[4,288,128]{2,1,0:T(8,128)(2,1)S(1)}, bf16[4,288,128]{2,1,0:T(8,128)(2,1)S(1)}, u32[]{:S(2)}, u32[]{:S(2)}) collective-permute-start(bf16[4,288,128]{2,1,0:T(8,128)(2,1)S(1)} %get-tuple-element.47), channel_id=1, source_target_pairs={{0,48},{16,0},{32,16},{48,32},{1,49},{17,1},{33,17},{49,33},{2,50}... | collective-permute-start | bytes 884744 | tf_op jit(solution)/shard_map/ppermute | solution.py:258
  65.7 12.2 %collective-permute-start.4 = (bf16[4,288,128]{2,1,0:T(8,128)(2,1)S(1)}, bf16[4,288,128]{2,1,0:T(8,128)(2,1)S(1)}, u32[]{:S(2)}, u32[]{:S(2)}) collective-permute-start(bf16[4,288,128]{2,1,0:T(8,128)(2,1)S(1)} %get-tuple-element.47), channel_id=1, source_target_pairs={{0,32},{16,48},{32,0},{48,16},{1,33},{17,49},{33,1},{49,17},{2,34}... | collective-permute-start | bytes 884744 | tf_op jit(solution)/shard_map/ppermute | solution.py:258
  68.7 10.0 %collective-permute-start.3 = (bf16[4,288,128]{2,1,0:T(8,128)(2,1)S(1)}, bf16[4,288,128]{2,1,0:T(8,128)(2,1)S(1)}, u32[]{:S(2)}, u32[]{:S(2)}) collective-permute-start(bf16[4,288,128]{2,1,0:T(8,128)(2,1)S(1)} %get-tuple-element.47), channel_id=1, source_target_pairs={{0,16},{16,32},{32,48},{48,0},{1,17},{17,33},{33,49},{49,1},{2,18}... | collective-permute-start | bytes 884744 | tf_op jit(solution)/shard_map/ppermute | solution.py:258
  72.8 12.5 %collective-permute-start.2 = (bf16[640,128]{1,0:T(8,128)(2,1)S(1)}, bf16[640,128]{1,0:T(8,128)(2,1)S(1)}, u32[]{:S(2)}, u32[]{:S(2)}) collective-permute-start(bf16[640,128]{1,0:T(8,128)(2,1)S(1)} %pad_maximum_fusion.2.mine), channel_id=1, source_target_pairs={{0,256},{256,0},{1,257},{257,1},{2,258},{258,2},{3,259},{259,3},{4... | collective-permute-start | bytes 491528 | tf_op jit(solution)/shard_map/ppermute | solution.py:249
  79.9 5.5 %collective-permute-start.6 = (bf16[16,288,128]{2,1,0:T(8,128)(2,1)}, bf16[16,288,128]{2,1,0:T(8,128)(2,1)}, u32[]{:S(2)}, u32[]{:S(2)}) collective-permute-start(bf16[16,288,128]{2,1,0:T(8,128)(2,1)} %bitcast.12), channel_id=1, source_target_pairs={{0,8},{8,0},{1,9},{9,1},{2,10},{10,2},{3,11},{11,3},{4,12},{12,4},... | collective-permute-start | bytes 3538952 | tf_op jit(solution)/shard_map/ppermute | solution.py:249
  81.9 3.4 %copy-start.2 = (f32[128]{0:T(128)S(1)}, f32[128]{0:T(128)}, u32[]{:S(2)}) copy-start(f32[128]{0:T(128)} %param.15) | copy-start | bytes 1540
  82.0 3.4 %copy-start.3 = (f32[128]{0:T(128)S(1)}, f32[128]{0:T(128)}, u32[]{:S(2)}) copy-start(f32[128]{0:T(128)} %param.16) | copy-start | bytes 1540
  88.1 1.0 copy-start
  89.1 5.9 %copy-start.4 = (bf16[256,128]{1,0:T(8,128)(2,1)S(1)}, bf16[256,128]{1,0:T(8,128)(2,1)}, u32[]{:S(2)}) copy-start(bf16[256,128]{1,0:T(8,128)(2,1)} %get-tuple-element.40.kept) | copy-start | bytes 196612
  89.1 25.4 %all-to-all-start.2 = ((bf16[4,1024,128]{2,1,0:T(8,128)(2,1)}), bf16[4,1024,128]{2,1,0:T(8,128)(2,1)S(1)}, u32[]{:S(2)}, u32[]{:S(2)}) async-start(bf16[4,1024,128]{2,1,0:T(8,128)(2,1)} %copy-done), calls=%async_computation.2 | async-start | bytes 2097152 | tf_op jit(solution)/shard_map/all_to_all | solution.py:308
  95.0 25.5 %copy-start.1 = (s32[128,128]{1,0:T(8,128)S(1)}, s32[128,128]{1,0:T(8,128)}, u32[]{:S(2)}) copy-start(s32[128,128]{1,0:T(8,128)} %bm_ref.1) | copy-start | bytes 196612
  114.5 15.4 %copy-start.8 = (f32[384]{0:T(512)S(1)}, f32[384]{0:T(512)}, u32[]{:S(2)}) copy-start(f32[384]{0:T(512)} %param.22) | copy-start | bytes 4612
  114.5 15.4 %copy-start.9 = (f32[384]{0:T(512)S(1)}, f32[384]{0:T(512)}, u32[]{:S(2)}) copy-start(f32[384]{0:T(512)} %param.23) | copy-start | bytes 4612
  114.5 6.0 %collective-permute-start.8 = (bf16[4,1024,128]{2,1,0:T(8,128)(2,1)S(1)}, bf16[4,1024,128]{2,1,0:T(8,128)(2,1)S(1)}, u32[]{:S(2)}, u32[]{:S(2)}) collective-permute-start(bf16[4,1024,128]{2,1,0:T(8,128)(2,1)S(1)} %all-to-all-done.2.q_ref.oown), channel_id=1, source_target_pairs={{0,8},{8,0},{1,9},{9,1},{2,10},{10,2},{3,11},{11,3},{4,12},{12,4},... | collective-permute-start | bytes 3145736 | tf_op jit(solution)/shard_map/ppermute | solution.py:249
  116.5 3.9 %collective-permute-start.7 = (bf16[4,512,128]{2,1,0:T(8,128)(2,1)S(1)}, bf16[4,512,128]{2,1,0:T(8,128)(2,1)S(1)}, u32[]{:S(2)}, u32[]{:S(2)}) collective-permute-start(bf16[4,512,128]{2,1,0:T(8,128)(2,1)S(1)} %bitcast.20), channel_id=1, source_target_pairs={{0,8},{8,0},{1,9},{9,1},{2,10},{10,2},{3,11},{11,3},{4,12},{12,4},... | collective-permute-start | bytes 1572872 | tf_op jit(solution)/shard_map/ppermute | solution.py:249
  125.1 11.7 %all-to-all-start.3 = ((bf16[4,208,256]{2,1,0:T(8,128)(2,1)}), bf16[4,208,256]{2,1,0:T(8,128)(2,1)S(1)}, u32[]{:S(2)}, u32[]{:S(2)}) async-start(bf16[4,208,256]{2,1,0:T(8,128)(2,1)} %attend.1), calls=%async_computation.3 | async-start | bytes 851968 | tf_op jit(solution)/shard_map/all_to_all | solution.py:320

commit v5 on v4

--- a/solution.py
+++ b/solution.py
@@ -178,21 +178,19 @@
         out = out + tn(kv[ch % 4, 256:, :], p.astype(BF))
     sums = jnp.concatenate(mass, axis=0)
     high = sums.astype(BF)
-    low = (sums - high.astype(F32)).astype(BF)
     rest = jnp.concatenate([*thirds(top), *thirds(total), jnp.zeros((10, 1024), F32)], axis=0).astype(BF)
     out = out.astype(BF)
     for i in range(4):
         cols = slice(i * 256, (i + 1) * 256)
         out_ref[i, :128, :] = out[:, cols]
         out_ref[i, 128:160, :] = high[:, cols]
-        out_ref[i, 160:192, :] = low[:, cols]
-        out_ref[i, 192:208, :] = rest[:, cols]
+        out_ref[i, 160:176, :] = rest[:, cols]
 
 
 def merge_kernel(parts, out_ref):
     c = lax.axis_index("c")
     hi = lax.Precision.HIGHEST
-    ends = [parts[i, 192:208, :].astype(F32) for i in range(4)]
+    ends = [parts[i, 160:176, :].astype(F32) for i in range(4)]
     tops = [e[0:1] + e[1:2] + e[2:3] for e in ends]
     top = jnp.maximum(jnp.maximum(tops[0], tops[1]), jnp.maximum(tops[2], tops[3]))
     factors = [jnp.exp2(t - top) for t in tops]
@@ -201,7 +199,7 @@
     out = sum(s * parts[i, :128, :].astype(F32) for i, s in enumerate(shares))
     att = out.T.astype(BF)
     mass = jnp.concatenate(
-        [s * (parts[i, 128:160, :].astype(F32) + parts[i, 160:192, :].astype(F32)) for i, s in enumerate(shares)], axis=0
+        [s * parts[i, 128:160, :].astype(F32) for i, s in enumerate(shares)], axis=0
     )
     i = lax.broadcasted_iota(jnp.int32, (128, 128), 0)
     b = lax.broadcasted_iota(jnp.int32, (128, 128), 1)
@@ -314,7 +312,7 @@
     kv1, ooth = lax.optimization_barrier((kv1, ooth))
 
     parts = call(
-        attend_kernel, sd((4, 208, 256), BF), 4, [pltpu.VMEM((2048, 1024), F32), pltpu.VMEM((32, 1024), F32)],
+        attend_kernel, sd((4, 176, 256), BF), 4, [pltpu.VMEM((2048, 1024), F32), pltpu.VMEM((32, 1024), F32)],
         limit=32, name="attend",
     )(qs, kv0, kv1, block_mask)
     parts = lax.all_to_all(parts, "x", 0, 0, tiled=True)

time: 175 us -> 174 us (level)
  no operation moved by 1% of the time
where the time goes in v5:
time: 174 us; the launch traced here: 171 us
  blocking collectives  81.6 us (47%)
  starting transfers between devices  59.8 us (34%)
  waiting for transfers between devices  12.6 us (7%)
  Pallas kernels  10.9 us (6%)
  local copies, waits for them, and re-layouts  3.43 us (2%)
  other arithmetic  2.12 us (1%)
    all_gather x1, blocking collectives, per_device(): toks = lax.all_gather(first, ('w', 'zh'), axis=0, tiled=False)  28.5 us
    ppermute x5, starting transfers between devices, swap(): return lax.ppermute(v, axis, [(0, 1), (1, 0)])  20.6 us
    all_gather x1, blocking collectives, per_device(): rows = lax.all_gather(done, ('w', 'zh'), axis=0, tiled=False)  20.1 us
    all_gather x1, blocking collectives, per_device(): kv0 = lax.all_gather(kv, 'zl', axis=0, tiled=False)  19.4 us
    all_to_all x2, starting transfers between devices, spread(): return lax.all_to_all(wide, axis, 0, 0, tiled=True)  17.3 us
    all_gather x1, blocking collectives, per_device(): lax.all_gather(lax.dynamic_slice_in_dim(rows, lax.axis_index('zh') * 128,...  13.5 us
    ppermute x3, starting transfers between devices, turn(): return lax.ppermute(v, axis, [(i, (i + k) % 4) for i in range(4)])  9.76 us
    all_to_all x1, waiting for transfers between devices, per_device(): parts = lax.all_to_all(parts, 'x', 0, 0, tiled=True)  6.16 us
  transfers between devices with their start and end apart: 13, of which 5 were waited for; matrix products, arithmetic and copies ran while one was open for 1% of the time, Pallas kernels for 0%

profile of v5, /device:TPU:6, one launch (start us, length us, event | category | flops | bytes accessed | tf_op | source)
XLA Modules:
  0.0 171.3 jit_solution(14307729567897398911)
XLA Ops:
  0.6 1.9 %prep.1 = (bf16[144,128]{1,0:T(8,128)(2,1)}, bf16[144,128]{1,0:T(8,128)(2,1)}, bf16[256,128]{1,0:T(8,128)(2,1)}, bf16[256,128]{1,0:T(8,128)(2,1)}, bf16[384,128]{1,0:T(8,128)(2,1)}, /*index=5*/bf16[96,128]{1,0:T(8,128)(2,1)}) custom-call(f32[2,2]{1,0:T(2,128)} %scale_h.1, s32[1,2]{1,0:T(1,128)} %bitcast.37, bf16[48,768]{1,0:T(8,128)(2,1)} %w_h.1, ...), custom_call_target="tpu_custom_call" | custom-call | tf_op jit(solution)/shard_map/prep/pallas_call | solution.py:265
  2.5 0.0 copy-start.5
  2.6 9.2 %collective-permute-start = (bf16[144,128]{1,0:T(8,128)(2,1)}, bf16[144,128]{1,0:T(8,128)(2,1)S(1)}, u32[]{:S(2)}, u32[]{:S(2)}) collective-permute-start(bf16[144,128]{1,0:T(8,128)(2,1)} %get-tuple-element.25), channel_id=1, source_target_pairs={{0,256},{256,0},{1,257},{257,1},{2,258},{258,2},{3,259},{259,3},{4... | collective-permute-start | bytes 110600 | tf_op jit(solution)/shard_map/ppermute | solution.py:247
  11.8 1.4 collective-permute-start.1
  13.2 0.0 collective-permute-done.1
  13.2 0.7 collective-permute-done
  13.9 0.8 pad_maximum_fusion.3
  14.7 0.8 broadcast_in_dim.27
  15.5 13.6 %all-to-all-start = ((bf16[4,384,128]{2,1,0:T(8,128)(2,1)}), bf16[4,384,128]{2,1,0:T(8,128)(2,1)S(1)}, u32[]{:S(2)}, u32[]{:S(2)}) async-start(bf16[4,384,128]{2,1,0:T(8,128)(2,1)} %broadcast_in_dim.27), calls=%async_computation | async-start | bytes 786432 | tf_op jit(solution)/shard_map/all_to_all | solution.py:252
  29.1 0.0 copy-done.5
  29.1 28.5 %all-gather = bf16[1536,128]{1,0:T(8,128)(2,1)S(1)} all-gather(bf16[384,128]{1,0:T(8,128)(2,1)S(1)} %copy-done.5), channel_id=2, replica_groups=mesh['zh'=2,'zl'=4,'x'=4,'c'=2,'w'=2,'y'=4] {'w','zh'}, dimensions={0}, use_global_device_ids=true | all-gather | bytes 491520 | tf_op jit(solution)/shard_map/all_gather | solution.py:287
  57.6 0.0 all-to-all-done
  57.6 1.5 broadcast_in_dim.28
  59.1 0.0 copy-start.7
  59.1 0.0 copy-start.6
  59.1 3.7 %all-to-all-start.1 = ((bf16[4,4,384,128]{3,2,1,0:T(8,128)(2,1)}), bf16[4,4,384,128]{3,2,1,0:T(8,128)(2,1)S(1)}, u32[]{:S(2)}, u32[]{:S(2)}) async-start(bf16[4,4,384,128]{3,2,1,0:T(8,128)(2,1)} %broadcast_in_dim.28), calls=%async_computation.1 | async-start | bytes 3145728 | tf_op jit(solution)/shard_map/all_to_all | solution.py:252
  62.8 0.1 slice_bitcast_fusion
  62.9 2.7 %collective-permute-start.5 = (bf16[4,288,128]{2,1,0:T(8,128)(2,1)S(1)}, bf16[4,288,128]{2,1,0:T(8,128)(2,1)S(1)}, u32[]{:S(2)}, u32[]{:S(2)}) collective-permute-start(bf16[4,288,128]{2,1,0:T(8,128)(2,1)S(1)} %get-tuple-element.47), channel_id=1, source_target_pairs={{0,48},{16,0},{32,16},{48,32},{1,49},{17,1},{33,17},{49,33},{2,50}... | collective-permute-start | bytes 884744 | tf_op jit(solution)/shard_map/ppermute | solution.py:256
  65.7 3.0 %collective-permute-start.4 = (bf16[4,288,128]{2,1,0:T(8,128)(2,1)S(1)}, bf16[4,288,128]{2,1,0:T(8,128)(2,1)S(1)}, u32[]{:S(2)}, u32[]{:S(2)}) collective-permute-start(bf16[4,288,128]{2,1,0:T(8,128)(2,1)S(1)} %get-tuple-element.47), channel_id=1, source_target_pairs={{0,32},{16,48},{32,0},{48,16},{1,33},{17,49},{33,1},{49,17},{2,34}... | collective-permute-start | bytes 884744 | tf_op jit(solution)/shard_map/ppermute | solution.py:256
  68.7 4.0 %collective-permute-start.3 = (bf16[4,288,128]{2,1,0:T(8,128)(2,1)S(1)}, bf16[4,288,128]{2,1,0:T(8,128)(2,1)S(1)}, u32[]{:S(2)}, u32[]{:S(2)}) collective-permute-start(bf16[4,288,128]{2,1,0:T(8,128)(2,1)S(1)} %get-tuple-element.47), channel_id=1, source_target_pairs={{0,16},{16,32},{32,48},{48,0},{1,17},{17,33},{33,49},{49,1},{2,18}... | collective-permute-start | bytes 884744 | tf_op jit(solution)/shard_map/ppermute | solution.py:256
  72.7 0.0 copy-done.7
  72.8 0.0 copy-done.6
  72.8 5.0 %collective-permute-start.2 = (bf16[640,128]{1,0:T(8,128)(2,1)S(1)}, bf16[640,128]{1,0:T(8,128)(2,1)S(1)}, u32[]{:S(2)}, u32[]{:S(2)}) collective-permute-start(bf16[640,128]{1,0:T(8,128)(2,1)S(1)} %pad_maximum_fusion.2.mine), channel_id=1, source_target_pairs={{0,256},{256,0},{1,257},{257,1},{2,258},{258,2},{3,259},{259,3},{4... | collective-permute-start | bytes 491528 | tf_op jit(solution)/shard_map/ppermute | solution.py:247
  77.8 0.0 collective-permute-done.5
  77.8 0.0 collective-permute-done.4
  77.8 0.8 collective-permute-done.3
  78.7 1.2 pad_maximum_fusion.1
  79.9 1.9 %collective-permute-start.6 = (bf16[16,288,128]{2,1,0:T(8,128)(2,1)}, bf16[16,288,128]{2,1,0:T(8,128)(2,1)}, u32[]{:S(2)}, u32[]{:S(2)}) collective-permute-start(bf16[16,288,128]{2,1,0:T(8,128)(2,1)} %bitcast.12), channel_id=1, source_target_pairs={{0,8},{8,0},{1,9},{9,1},{2,10},{10,2},{3,11},{11,3},{4,12},{12,4},... | collective-permute-start | bytes 3538952 | tf_op jit(solution)/shard_map/ppermute | solution.py:247
  81.8 0.2 pad_maximum_fusion.wown
  81.9 0.0 copy-start.2
  82.0 0.0 copy-start.3
  82.0 3.4 %collective-permute-done.2.theirs = bf16[640,128]{1,0:T(8,128)(2,1)S(1)} collective-permute-done((bf16[640,128]{1,0:T(8,128)(2,1)S(1)}, bf16[640,128]{1,0:T(8,128)(2,1)S(1)}, u32[]{:S(2)}, u32[]{:S(2)}) %collective-permute-start.2) | collective-permute-done | bytes 163872 | tf_op jit(solution)/shard_map/ppermute | solution.py:247
  85.3 0.0 all-to-all-done.1.xs
  85.3 0.0 collective-permute-done.6
  85.3 0.0 copy-done.2
  85.4 0.0 copy-done.3
  85.4 2.7 %project.1 = (bf16[4,1024,128]{2,1,0:T(8,128)(2,1)S(1)}, bf16[512,128]{1,0:T(8,128)(2,1)S(1)}) custom-call(bf16[4,4,384,128]{3,2,1,0:T(8,128)(2,1)S(1)} %all-to-all-done.1.xs, bf16[4,4,2,144,128]{4,3,2,1,0:T(8,128)(2,1)S(1)} %pad_maximum_fusion.wown, bf16[4,4,2,144,128]{4,3,2,1,0:T(8,128)(2,1)} %bitcast.13.woth, f32[1,384]{1,0:T(1,128)S(1)} %bias.1, ...), custom_call_target="tpu_custom_call" | custom-call | tf_op jit(solution)/shard_map/project/pallas_call | solution.py:301
  88.1 0.0 copy-start
  88.1 1.0 copy-done
  89.1 0.0 copy-start.4
  89.1 5.9 %all-to-all-start.2 = ((bf16[4,1024,128]{2,1,0:T(8,128)(2,1)}), bf16[4,1024,128]{2,1,0:T(8,128)(2,1)S(1)}, u32[]{:S(2)}, u32[]{:S(2)}) async-start(bf16[4,1024,128]{2,1,0:T(8,128)(2,1)} %copy-done), calls=%async_computation.2 | async-start | bytes 2097152 | tf_op jit(solution)/shard_map/all_to_all | solution.py:306
  95.0 0.0 copy-done.4
  95.0 0.0 copy-start.1
  95.0 0.1 select.1
  95.0 19.4 %all-gather.1 = bf16[2048,128]{1,0:T(8,128)(2,1)S(1)} all-gather(bf16[512,128]{1,0:T(8,128)(2,1)S(1)} %select.1), channel_id=3, replica_groups=mesh['zh'=2,'zl'=4,'x'=4,'c'=2,'w'=2,'y'=4] {'zl'}, dimensions={0}, use_global_device_ids=true | all-gather | bytes 655360 | tf_op jit(solution)/shard_map/all_gather | solution.py:308
  114.4 0.0 all-to-all-done.2.q_ref.oown
  114.5 0.0 copy-start.8
  114.5 0.0 copy-start.9
  114.5 2.0 %collective-permute-start.8 = (bf16[4,1024,128]{2,1,0:T(8,128)(2,1)S(1)}, bf16[4,1024,128]{2,1,0:T(8,128)(2,1)S(1)}, u32[]{:S(2)}, u32[]{:S(2)}) collective-permute-start(bf16[4,1024,128]{2,1,0:T(8,128)(2,1)S(1)} %all-to-all-done.2.q_ref.oown), channel_id=1, source_target_pairs={{0,8},{8,0},{1,9},{9,1},{2,10},{10,2},{3,11},{11,3},{4,12},{12,4},... | collective-permute-start | bytes 3145736 | tf_op jit(solution)/shard_map/ppermute | solution.py:247
  116.5 2.4 %collective-permute-start.7 = (bf16[4,512,128]{2,1,0:T(8,128)(2,1)S(1)}, bf16[4,512,128]{2,1,0:T(8,128)(2,1)S(1)}, u32[]{:S(2)}, u32[]{:S(2)}) collective-permute-start(bf16[4,512,128]{2,1,0:T(8,128)(2,1)S(1)} %bitcast.20), channel_id=1, source_target_pairs={{0,8},{8,0},{1,9},{9,1},{2,10},{10,2},{3,11},{11,3},{4,12},{12,4},... | collective-permute-start | bytes 1572872 | tf_op jit(solution)/shard_map/ppermute | solution.py:247
  118.9 1.5 collective-permute-done.7.kv1
  120.4 0.0 collective-permute-done.8.ooth
  120.4 0.0 copy-done.1
  120.4 4.5 %attend.1 = bf16[4,176,256]{2,1,0:T(8,128)(2,1)} custom-call(bf16[4,1024,128]{2,1,0:T(8,128)(2,1)S(1)} %all-to-all-done.2.q_ref.oown, bf16[4,512,128]{2,1,0:T(8,128)(2,1)S(1)} %bitcast.21, bf16[4,512,128]{2,1,0:T(8,128)(2,1)S(1)} %collective-permute-done.7.kv1, s32[128,128]{1,0:T(8,128)S(1)} %copy-done.1), custom_call_target="tpu_custom_call" | custom-call | tf_op jit(solution)/shard_map/attend/pallas_call | solution.py:314
  125.0 4.8 %all-to-all-start.3 = ((bf16[4,176,256]{2,1,0:T(8,128)(2,1)}), bf16[4,176,256]{2,1,0:T(8,128)(2,1)S(1)}, u32[]{:S(2)}, u32[]{:S(2)}) async-start(bf16[4,176,256]{2,1,0:T(8,128)(2,1)} %attend.1), calls=%async_computation.3 | async-start | bytes 720896 | tf_op jit(solution)/shard_map/all_to_all | solution.py:318
  129.8 0.0 copy-done.8
  129.8 0.0 copy-done.9
  129.8 6.2 %all-to-all-done.3.parts = bf16[4,176,256]{2,1,0:T(8,128)(2,1)S(1)} async-done(((bf16[4,176,256]{2,1,0:T(8,128)(2,1)}), bf16[4,176,256]{2,1,0:T(8,128)(2,1)S(1)}, u32[]{:S(2)}, u32[]{:S(2)}) %all-to-all-start.3) | async-done | bytes 360480 | tf_op jit(solution)/shard_map/all_to_all | solution.py:318
  136.0 0.5 merge.1
  136.4 20.1 %all-gather.2 = bf16[1088,128]{1,0:T(8,128)(2,1)S(1)} all-gather(bf16[272,128]{1,0:T(8,128)(2,1)S(1)} %merge.1), channel_id=4, replica_groups=mesh['zh'=2,'zl'=4,'x'=4,'c'=2,'w'=2,'y'=4] {'w','zh'}, dimensions={0}, use_global_device_ids=true | all-gather | bytes 348160 | tf_op jit(solution)/shard_map/all_gather | solution.py:320
  156.6 13.5 %all-gather.3 = bf16[16,128,128]{2,1,0:T(8,128)(2,1)S(1)} all-gather(bf16[4,128,128]{2,1,0:T(8,128)(2,1)S(1)} %constant_dynamic-slice_fusion), channel_id=5, replica_groups=mesh['zh'=2,'zl'=4,'x'=4,'c'=2,'w'=2,'y'=4] {'y'}, dimensions={0}, use_global_device_ids=true | all-gather | bytes 655360 | tf_op jit(solution)/shard_map/all_gather | solution.py:321
  170.1 1.3 finish.1
  (7 shorter events, 0.0 us)
Async XLA Ops:
  2.5 26.6 %copy-start.5 = (bf16[384,128]{1,0:T(8,128)(2,1)S(1)}, bf16[384,128]{1,0:T(8,128)(2,1)}, u32[]{:S(2)}) copy-start(bf16[384,128]{1,0:T(8,128)(2,1)} %get-tuple-element.29) | copy-start | bytes 294916
  2.6 11.4 %collective-permute-start = (bf16[144,128]{1,0:T(8,128)(2,1)}, bf16[144,128]{1,0:T(8,128)(2,1)S(1)}, u32[]{:S(2)}, u32[]{:S(2)}) collective-permute-start(bf16[144,128]{1,0:T(8,128)(2,1)} %get-tuple-element.25), channel_id=1, source_target_pairs={{0,256},{256,0},{1,257},{257,1},{2,258},{258,2},{3,259},{259,3},{4... | collective-permute-start | bytes 110600 | tf_op jit(solution)/shard_map/ppermute | solution.py:247
  11.8 1.4 collective-permute-start.1
  15.5 42.1 %all-to-all-start = ((bf16[4,384,128]{2,1,0:T(8,128)(2,1)}), bf16[4,384,128]{2,1,0:T(8,128)(2,1)S(1)}, u32[]{:S(2)}, u32[]{:S(2)}) async-start(bf16[4,384,128]{2,1,0:T(8,128)(2,1)} %broadcast_in_dim.27), calls=%async_computation | async-start | bytes 786432 | tf_op jit(solution)/shard_map/all_to_all | solution.py:252
  59.1 13.6 %copy-start.7 = (f32[768]{0:T(1024)S(1)}, f32[768]{0:T(1024)}, u32[]{:S(2)}) copy-start(f32[768]{0:T(1024)} %param.14) | copy-start | bytes 9220
  59.1 13.6 %copy-start.6 = (bf16[256,128]{1,0:T(8,128)(2,1)S(1)}, bf16[256,128]{1,0:T(8,128)(2,1)}, u32[]{:S(2)}) copy-start(bf16[256,128]{1,0:T(8,128)(2,1)} %get-tuple-element.32) | copy-start | bytes 196612
  59.1 26.2 %all-to-all-start.1 = ((bf16[4,4,384,128]{3,2,1,0:T(8,128)(2,1)}), bf16[4,4,384,128]{3,2,1,0:T(8,128)(2,1)S(1)}, u32[]{:S(2)}, u32[]{:S(2)}) async-start(bf16[4,4,384,128]{3,2,1,0:T(8,128)(2,1)} %broadcast_in_dim.28), calls=%async_computation.1 | async-start | bytes 3145728 | tf_op jit(solution)/shard_map/all_to_all | solution.py:252
  62.9 14.9 %collective-permute-start.5 = (bf16[4,288,128]{2,1,0:T(8,128)(2,1)S(1)}, bf16[4,288,128]{2,1,0:T(8,128)(2,1)S(1)}, u32[]{:S(2)}, u32[]{:S(2)}) collective-permute-start(bf16[4,288,128]{2,1,0:T(8,128)(2,1)S(1)} %get-tuple-element.47), channel_id=1, source_target_pairs={{0,48},{16,0},{32,16},{48,32},{1,49},{17,1},{33,17},{49,33},{2,50}... | collective-permute-start | bytes 884744 | tf_op jit(solution)/shard_map/ppermute | solution.py:256
  65.7 12.2 %collective-permute-start.4 = (bf16[4,288,128]{2,1,0:T(8,128)(2,1)S(1)}, bf16[4,288,128]{2,1,0:T(8,128)(2,1)S(1)}, u32[]{:S(2)}, u32[]{:S(2)}) collective-permute-start(bf16[4,288,128]{2,1,0:T(8,128)(2,1)S(1)} %get-tuple-element.47), channel_id=1, source_target_pairs={{0,32},{16,48},{32,0},{48,16},{1,33},{17,49},{33,1},{49,17},{2,34}... | collective-permute-start | bytes 884744 | tf_op jit(solution)/shard_map/ppermute | solution.py:256
  68.7 10.0 %collective-permute-start.3 = (bf16[4,288,128]{2,1,0:T(8,128)(2,1)S(1)}, bf16[4,288,128]{2,1,0:T(8,128)(2,1)S(1)}, u32[]{:S(2)}, u32[]{:S(2)}) collective-permute-start(bf16[4,288,128]{2,1,0:T(8,128)(2,1)S(1)} %get-tuple-element.47), channel_id=1, source_target_pairs={{0,16},{16,32},{32,48},{48,0},{1,17},{17,33},{33,49},{49,1},{2,18}... | collective-permute-start | bytes 884744 | tf_op jit(solution)/shard_map/ppermute | solution.py:256
  72.8 12.5 %collective-permute-start.2 = (bf16[640,128]{1,0:T(8,128)(2,1)S(1)}, bf16[640,128]{1,0:T(8,128)(2,1)S(1)}, u32[]{:S(2)}, u32[]{:S(2)}) collective-permute-start(bf16[640,128]{1,0:T(8,128)(2,1)S(1)} %pad_maximum_fusion.2.mine), channel_id=1, source_target_pairs={{0,256},{256,0},{1,257},{257,1},{2,258},{258,2},{3,259},{259,3},{4... | collective-permute-start | bytes 491528 | tf_op jit(solution)/shard_map/ppermute | solution.py:247
  79.9 5.5 %collective-permute-start.6 = (bf16[16,288,128]{2,1,0:T(8,128)(2,1)}, bf16[16,288,128]{2,1,0:T(8,128)(2,1)}, u32[]{:S(2)}, u32[]{:S(2)}) collective-permute-start(bf16[16,288,128]{2,1,0:T(8,128)(2,1)} %bitcast.12), channel_id=1, source_target_pairs={{0,8},{8,0},{1,9},{9,1},{2,10},{10,2},{3,11},{11,3},{4,12},{12,4},... | collective-permute-start | bytes 3538952 | tf_op jit(solution)/shard_map/ppermute | solution.py:247
  81.9 3.4 %copy-start.2 = (f32[128]{0:T(128)S(1)}, f32[128]{0:T(128)}, u32[]{:S(2)}) copy-start(f32[128]{0:T(128)} %param.15) | copy-start | bytes 1540
  82.0 3.4 %copy-start.3 = (f32[128]{0:T(128)S(1)}, f32[128]{0:T(128)}, u32[]{:S(2)}) copy-start(f32[128]{0:T(128)} %param.16) | copy-start | bytes 1540
  88.1 1.0 copy-start
  89.1 5.9 %copy-start.4 = (bf16[256,128]{1,0:T(8,128)(2,1)S(1)}, bf16[256,128]{1,0:T(8,128)(2,1)}, u32[]{:S(2)}) copy-start(bf16[256,128]{1,0:T(8,128)(2,1)} %get-tuple-element.40.kept) | copy-start | bytes 196612
  89.1 25.4 %all-to-all-start.2 = ((bf16[4,1024,128]{2,1,0:T(8,128)(2,1)}), bf16[4,1024,128]{2,1,0:T(8,128)(2,1)S(1)}, u32[]{:S(2)}, u32[]{:S(2)}) async-start(bf16[4,1024,128]{2,1,0:T(8,128)(2,1)} %copy-done), calls=%async_computation.2 | async-start | bytes 2097152 | tf_op jit(solution)/shard_map/all_to_all | solution.py:306
  95.0 25.5 %copy-start.1 = (s32[128,128]{1,0:T(8,128)S(1)}, s32[128,128]{1,0:T(8,128)}, u32[]{:S(2)}) copy-start(s32[128,128]{1,0:T(8,128)} %bm_ref.1) | copy-start | bytes 196612
  114.5 15.3 %copy-start.8 = (f32[384]{0:T(512)S(1)}, f32[384]{0:T(512)}, u32[]{:S(2)}) copy-start(f32[384]{0:T(512)} %param.22) | copy-start | bytes 4612
  114.5 15.3 %copy-start.9 = (f32[384]{0:T(512)S(1)}, f32[384]{0:T(512)}, u32[]{:S(2)}) copy-start(f32[384]{0:T(512)} %param.23) | copy-start | bytes 4612
  114.5 6.0 %collective-permute-start.8 = (bf16[4,1024,128]{2,1,0:T(8,128)(2,1)S(1)}, bf16[4,1024,128]{2,1,0:T(8,128)(2,1)S(1)}, u32[]{:S(2)}, u32[]{:S(2)}) collective-permute-start(bf16[4,1024,128]{2,1,0:T(8,128)(2,1)S(1)} %all-to-all-done.2.q_ref.oown), channel_id=1, source_target_pairs={{0,8},{8,0},{1,9},{9,1},{2,10},{10,2},{3,11},{11,3},{4,12},{12,4},... | collective-permute-start | bytes 3145736 | tf_op jit(solution)/shard_map/ppermute | solution.py:247
  116.5 3.9 %collective-permute-start.7 = (bf16[4,512,128]{2,1,0:T(8,128)(2,1)S(1)}, bf16[4,512,128]{2,1,0:T(8,128)(2,1)S(1)}, u32[]{:S(2)}, u32[]{:S(2)}) collective-permute-start(bf16[4,512,128]{2,1,0:T(8,128)(2,1)S(1)} %bitcast.20), channel_id=1, source_target_pairs={{0,8},{8,0},{1,9},{9,1},{2,10},{10,2},{3,11},{11,3},{4,12},{12,4},... | collective-permute-start | bytes 1572872 | tf_op jit(solution)/shard_map/ppermute | solution.py:247
  125.0 11.0 %all-to-all-start.3 = ((bf16[4,176,256]{2,1,0:T(8,128)(2,1)}), bf16[4,176,256]{2,1,0:T(8,128)(2,1)S(1)}, u32[]{:S(2)}, u32[]{:S(2)}) async-start(bf16[4,176,256]{2,1,0:T(8,128)(2,1)} %attend.1), calls=%async_computation.3 | async-start | bytes 720896 | tf_op jit(solution)/shard_map/all_to_all | solution.py:318
